TPU v7x, 128 devices: a whole 4x4x4 slice. The times are simulated.
128 devices in a mesh: dp: 16 (over y, z), group: 8 (over x, core).
Axes of the slice: x: 4, y: 4, z: 4, core: 2. Of those that a mesh axis runs over, the one named last changes fastest.
Arguments:
- grad_partial: bfloat16 [16, 56, 1024, 1024], P('dp', 'group')
- left_root: bfloat16 [256, 1024, 1024], P(('dp', 'group'))
- right_root: bfloat16 [256, 1024, 1024], P(('dp', 'group'))
- block_owner: int32 [56], replicated, may hold values from 0 to 255, as said below
- momentum: float32 [56, 1024, 1024], P('group', 'dp'), may hold values from -6 to 6
Outputs:
- new_momentum: float32 [56, 1024, 1024], P('group', 'dp')
Inputs may be any that keep to these rules, and one draw needn't show every extreme that they name: `block_owner`: distinct values. A value v names slot v % 2 of the device whose index over dp and group, dp slowest, is v // 2. Block b belongs to index b // 7 of group. The 7 blocks of each index of group go 4 to one owner group common to all indices and one each to 3 different other owner groups; no device holds two blocks of the same index of group; the common owner group holds 32 blocks.
All inputs are finite; a program needn't handle non-finite values.
Results may differ from a plain program's by a relative error of at most 0.018.
Values may be sent and summed in bfloat16 or wider, within the bound.
No kernel may reach another device: no remote copies, remote signals or barrier semaphores. Data moves between devices by JAX's collectives and lax.ppermute only.
A program may use at most 128 MiB of HBM per device.

v0:
```python
import jax
import jax.numpy as jnp
from jax import lax
from jax.sharding import PartitionSpec as P

CAPG = 4


def shards(grad_partial, left_root, right_root, block_owner, momentum):
    summed = lax.psum_scatter(grad_partial, "dp", scatter_dimension=2, tiled=True).astype(
        jnp.float32
    )
    grad_rows = summed[0].astype(jnp.bfloat16)
    dp_count = lax.axis_size("dp")
    group_count = lax.axis_size("group")
    dp_index = lax.axis_index("dp")
    group_index = lax.axis_index("group")
    local_count, row_count, col_count = grad_rows.shape
    slot_count = left_root.shape[0]
    block_total = block_owner.shape[0]
    block_ids = jnp.arange(block_total, dtype=jnp.int32)
    owner_device = block_owner // slot_count
    owner_group = owner_device % group_count
    owner_place = owner_device // group_count * slot_count + block_owner % slot_count
    source_group = block_ids // local_count
    earlier = (
        (block_ids[None, :] < block_ids[:, None])
        & (source_group[None, :] == source_group[:, None])
        & (owner_group[None, :] == owner_group[:, None])
    )
    rank_in = jnp.sum(earlier.astype(jnp.int32), axis=1)
    buffer_size = group_count * CAPG
    column = source_group * CAPG + rank_in
    mine_target = lax.dynamic_slice_in_dim(
        owner_group * CAPG + rank_in, group_index * local_count, local_count
    )
    selector = (mine_target[None, :] == jnp.arange(buffer_size, dtype=jnp.int32)[:, None]).astype(
        jnp.bfloat16
    )
    held_here = owner_group == group_index
    place_match = (
        (owner_place[None, :] == jnp.arange(dp_count * slot_count, dtype=jnp.int32)[:, None])
        & held_here[None, :]
    ).astype(jnp.float32)
    column_match = (column[:, None] == jnp.arange(buffer_size, dtype=jnp.int32)[None, :]).astype(
        jnp.float32
    )
    arrangement = jnp.dot(place_match, column_match).astype(jnp.bfloat16)
    device_count = dp_count * group_count
    self_device = dp_index * group_count + group_index
    mine_device = lax.dynamic_slice_in_dim(owner_device, group_index * local_count, local_count)
    picker = (mine_device[None, :] == jnp.arange(device_count, dtype=jnp.int32)[:, None]).astype(
        jnp.bfloat16
    )
    outgoing = jnp.einsum(
        "oj,jrw->orw", picker, grad_rows, preferred_element_type=jnp.float32
    ).astype(jnp.bfloat16)
    outgoing = outgoing.reshape(device_count, 1, row_count, col_count)
    incoming = lax.all_to_all(outgoing, ("dp", "group"), split_axis=0, concat_axis=1, tiled=True)
    held_mine = owner_device == self_device
    slot_source = (
        ((block_owner % slot_count)[None, :] == jnp.arange(slot_count, dtype=jnp.int32)[:, None])
        & held_mine[None, :]
    ).astype(jnp.float32)
    group_hit = (source_group[:, None] == jnp.arange(group_count, dtype=jnp.int32)[None, :]).astype(
        jnp.float32
    )
    source_pick = jnp.dot(slot_source, group_hit).astype(jnp.bfloat16)
    pieces = incoming.reshape(dp_count, group_count, row_count, col_count)
    blocks_full = jnp.einsum(
        "sg,dgrw->sdrw", source_pick, pieces, preferred_element_type=jnp.float32
    ).astype(jnp.bfloat16)
    blocks_full = blocks_full.reshape(slot_count, dp_count * row_count, col_count)
    left_part = jnp.einsum(
        "sij,sjk->sik", left_root, blocks_full, preferred_element_type=jnp.float32
    ).astype(jnp.bfloat16)
    product = jnp.einsum("sij,sjk->sik", left_part, right_root, preferred_element_type=jnp.float32)
    grad_norm = jnp.sqrt(jnp.mean(jnp.square(blocks_full.astype(jnp.float32)), axis=(1, 2)))
    prod_norm = jnp.sqrt(jnp.mean(product * product, axis=(1, 2)) + 1e-06)
    direction = (product * (grad_norm / prod_norm)[:, None, None]).astype(jnp.bfloat16)
    returned = lax.all_to_all(direction, "dp", split_axis=1, concat_axis=0, tiled=True)
    regrouped = jnp.einsum(
        "qc,qrw->crw", arrangement, returned, preferred_element_type=jnp.float32
    ).astype(jnp.bfloat16)
    regrouped = regrouped.reshape(group_count, CAPG, row_count, col_count)
    arrived = lax.all_to_all(regrouped, "group", split_axis=0, concat_axis=0, tiled=True)
    direction_rows = jnp.einsum(
        "cj,crw->jrw",
        selector,
        arrived.reshape(buffer_size, row_count, col_count),
        preferred_element_type=jnp.float32,
    )
    return 0.9 * momentum + direction_rows


def solution(mesh):
    return jax.shard_map(
        shards,
        mesh=mesh,
        in_specs=(
            P("dp", "group", None, None),
            P(("dp", "group"), None, None),
            P(("dp", "group"), None, None),
            P(),
            P("group", "dp", None),
        ),
        out_specs=P("group", "dp", None),
        check_vma=False,
    )
```

profile of v0, /device:TPU:0, one launch (start us, length us, event | category | flops | bytes accessed | tf_op | source)
XLA Modules:
  0.0 623.1 jit_solution(6885482065759726955)
XLA Ops:
  6.5 0.0 copy-start.1
  6.5 0.0 reduce-scatter.2.cloned.1.call-start
  6.5 0.7 reduce-scatter.2.cloned.1.call-update
  7.3 0.0 copy-done.1
  7.3 0.1 dynamic_slice.7
  7.4 107.8 %reduce-scatter.2.cloned.1.call-done = bf16[1,7,64,1024]{3,2,1,0:T(8,128)(2,1)} async-done(((bf16[1,7,1024,1024]{3,2,1,0:T(8,128)(2,1)}), bf16[1,7,64,1024]{3,2,1,0:T(8,128)(2,1)}) %reduce-scatter.2.cloned.1.call-update) | async-done | bytes 917520 | tf_op jit(solution)/shard_map/reduce_scatter | solution.py:10
  115.2 11.5 %convert_bitcast_fusion = bf16[128,1,64,1024]{3,0,2,1:T(8,128)(2,1)} fusion(bf16[7,64,1024]{2,1,0:T(8,128)(2,1)} %bitcast.38, s32[7]{0:T(128)S(1)} %dynamic_slice.7), kind=kOutput, calls=%fused_computation.2 | convolution fusion | flops 125830016 | bytes 17694748 | tf_op jit(solution)/shard_map/oj,jrw->orw/dot_general | solution.py:55
  126.7 18.7 %copy.44 = bf16[128,1,64,1024]{3,2,1,0:T(8,128)(2,1)} copy(bf16[128,1,64,1024]{3,0,2,1:T(8,128)(2,1)} %convert_bitcast_fusion) | data formatting | bytes 33554432 | tf_op jit(solution)/shard_map/reshape | solution.py:58
  145.4 8.2 %all-to-all-start = ((bf16[128,1,64,1024]{3,2,1,0:T(8,128)(2,1)}), bf16[128,1,64,1024]{3,2,1,0:T(8,128)(2,1)}, u32[]{:S(2)}, u32[]{:S(2)}) async-start(bf16[128,1,64,1024]{3,2,1,0:T(8,128)(2,1)} %copy.44), calls=%async_computation.1 | async-start | bytes 33554432 | tf_op jit(solution)/shard_map/all_to_all | solution.py:59
  153.6 226.2 %all-to-all-done = bf16[128,1,64,1024]{3,2,1,0:T(8,128)(2,1)} async-done(((bf16[128,1,64,1024]{3,2,1,0:T(8,128)(2,1)}), bf16[128,1,64,1024]{3,2,1,0:T(8,128)(2,1)}, u32[]{:S(2)}, u32[]{:S(2)}) %all-to-all-start) | async-done | bytes 16777248 | tf_op jit(solution)/shard_map/all_to_all | solution.py:59
  379.9 18.5 %multiply_reduce_fusion.1 = (f32[2]{0:T(128)S(1)}, bf16[2,16,64,1024]{3,0,2,1:T(2,128)(2,1)}) fusion(bf16[16,8,64,1024]{3,2,1,0:T(8,128)(2,1)} %bitcast.7, s32[56]{0:T(128)S(1)} %get-tuple-element.16, pred[56]{0:T(512)(128)(4,1)S(1)} %broadcast_compare_fusion, s32[56]{0:T(128)S(1)} %get-tuple-element.9), kind=kOutput, calls=%fused_computation.5 | convolution fusion | flops 41945520 | bytes 20972032 | tf_op jit(solution)/shard_map/sg,dgrw->sdrw/dot_general | solution.py:70
  398.3 17.7 %multiply_reduce_fusion = (f32[2]{0:T(128)S(1)}, f32[2,1024,1024]{2,1,0:T(8,128)}) fusion(bf16[2,1024,1024]{2,1,0:T(8,128)(2,1)} %param.7, bf16[2,1024,1024]{2,1,0:T(8,128)(2,1)} %param.6, bf16[2,1024,1024]{2,0,1:T(2,128)(2,1)} %bitcast.39), kind=kOutput, calls=%fused_computation.4 | convolution fusion | flops 8596226048 | bytes 20971528 | tf_op jit(solution)/shard_map/sij,sjk->sik/dot_general | solution.py:77
  416.0 4.7 multiply_convert_fusion
  420.7 6.3 %copy.48 = bf16[2,1024,1024]{2,0,1:T(2,128)(2,1)} copy(bf16[2,1024,1024]{2,1,0:T(8,128)(2,1)S(1)} %multiply_convert_fusion) | data formatting | bytes 8388608 | tf_op jit(solution)/shard_map/convert_element_type | solution.py:80
  427.0 19.0 %all-to-all-start.1 = ((bf16[2,1024,1024]{2,0,1:T(2,128)(2,1)}), bf16[2,1024,1024]{2,0,1:T(2,128)(2,1)}, u32[]{:S(2)}, u32[]{:S(2)}) async-start(bf16[2,1024,1024]{2,0,1:T(2,128)(2,1)} %copy.48), calls=%async_computation.2 | async-start | bytes 8388608 | tf_op jit(solution)/shard_map/all_to_all | solution.py:81
  446.0 0.2 convert_reduce_fusion
  446.2 60.8 %all-to-all-done.1 = bf16[2,1024,1024]{2,0,1:T(2,128)(2,1)} async-done(((bf16[2,1024,1024]{2,0,1:T(2,128)(2,1)}), bf16[2,1024,1024]{2,0,1:T(2,128)(2,1)}, u32[]{:S(2)}, u32[]{:S(2)}) %all-to-all-start.1) | async-done | bytes 4194336 | tf_op jit(solution)/shard_map/all_to_all | solution.py:81
  507.0 8.8 %copy.76 = bf16[2,16,64,1024]{3,0,1,2:T(2,128)(2,1)} copy(bf16[2,16,64,1024]{3,0,2,1:T(2,128)(2,1)} %bitcast.9) | data formatting | bytes 8388608 | tf_op jit(solution)/shard_map/all_to_all | solution.py:81
  515.7 7.2 %all_to_all.27 = bf16[32,64,1024]{2,0,1:T(8,128)(2,1)} reshape(bf16[16,2,64,1024]{3,1,0,2:T(2,128)(2,1)} %bitcast.37) | data formatting | bytes 8388608 | tf_op jit(solution)/shard_map/all_to_all | solution.py:81
  522.9 5.6 convolution_convert_fusion
  528.6 7.2 %reshape.73 = bf16[8,4,64,1024]{3,1,0,2:T(4,128)(2,1)} reshape(bf16[32,64,1024]{2,0,1:T(8,128)(2,1)} %convolution_convert_fusion) | data formatting | bytes 8388608 | tf_op jit(solution)/shard_map/reshape | solution.py:85
  535.8 5.9 copy.51
  541.6 5.3 all-to-all-start.2
  546.9 0.1 dynamic_slice.6
  547.0 49.7 %all-to-all-done.2 = bf16[8,4,64,1024]{3,1,2,0:T(4,128)(2,1)} async-done(((bf16[8,4,64,1024]{3,1,2,0:T(4,128)(2,1)}), bf16[8,4,64,1024]{3,1,2,0:T(4,128)(2,1)}, u32[]{:S(2)}, u32[]{:S(2)}) %all-to-all-start.2) | async-done | bytes 4194336 | tf_op jit(solution)/shard_map/all_to_all | solution.py:86
  596.7 6.6 %copy.52 = bf16[8,4,64,1024]{3,1,0,2:T(4,128)(2,1)} copy(bf16[8,4,64,1024]{3,1,2,0:T(4,128)(2,1)} %all-to-all-done.2) | data formatting | bytes 8388608 | tf_op jit(solution)/shard_map/all_to_all | solution.py:86
  603.3 6.9 %reshape.74 = bf16[32,64,1024]{2,0,1:T(8,128)(2,1)} reshape(bf16[8,4,64,1024]{3,1,0,2:T(4,128)(2,1)} %copy.52) | data formatting | bytes 8388608 | tf_op jit(solution)/shard_map/reshape | solution.py:90
  610.2 0.0 copy-start
  610.2 3.0 fusion.30
  613.3 0.0 copy-done
  613.3 2.5 copy_add_fusion
  (5 shorter events, 0.1 us)
Async XLA Ops:
  6.5 0.7 copy-start.1
  6.5 108.6 %reduce-scatter.2.cloned.1.call-start = ((), (), s32[]{:S(2)}) async-start(), calls=%async_computation.4 | async-start | bytes 15597568 | tf_op jit(solution)/shard_map/reduce_scatter | solution.py:10
  145.4 234.5 %all-to-all-start = ((bf16[128,1,64,1024]{3,2,1,0:T(8,128)(2,1)}), bf16[128,1,64,1024]{3,2,1,0:T(8,128)(2,1)}, u32[]{:S(2)}, u32[]{:S(2)}) async-start(bf16[128,1,64,1024]{3,2,1,0:T(8,128)(2,1)} %copy.44), calls=%async_computation.1 | async-start | bytes 33554432 | tf_op jit(solution)/shard_map/all_to_all | solution.py:59
  427.0 80.0 %all-to-all-start.1 = ((bf16[2,1024,1024]{2,0,1:T(2,128)(2,1)}), bf16[2,1024,1024]{2,0,1:T(2,128)(2,1)}, u32[]{:S(2)}, u32[]{:S(2)}) async-start(bf16[2,1024,1024]{2,0,1:T(2,128)(2,1)} %copy.48), calls=%async_computation.2 | async-start | bytes 8388608 | tf_op jit(solution)/shard_map/all_to_all | solution.py:81
  541.6 55.1 %all-to-all-start.2 = ((bf16[8,4,64,1024]{3,1,2,0:T(4,128)(2,1)}), bf16[8,4,64,1024]{3,1,2,0:T(4,128)(2,1)}, u32[]{:S(2)}, u32[]{:S(2)}) async-start(bf16[8,4,64,1024]{3,1,2,0:T(4,128)(2,1)} %copy.51), calls=%async_computation.3 | async-start | bytes 8388608 | tf_op jit(solution)/shard_map/all_to_all | solution.py:86
  610.2 3.0 copy-start
Sparse Core Ops, SparseCore 0:
  10.8 104.3 reduce-scatter.1
where the time goes:
time: 632 us; the launch traced here: 623 us
  waiting for transfers between devices  445 us (70%)
  local copies, waits for them, and re-layouts  67.7 us (11%)
  matrix products  56.4 us (9%)
  starting transfers between devices  32.4 us (5%)
  between operations  13.9 us (2%)
  other arithmetic  7.46 us (1%)
    all_to_all x1, waiting for transfers between devices, shards(): lax.all_to_all(outgoing, ('dp', 'group'), split_axis=0, concat_axis=1, ti...  226 us
    reduce_scatter x1, waiting for transfers between devices, shards(): lax.psum_scatter(grad_partial, 'dp', scatter_dimension=2, tiled=True)  108 us
    all_to_all x1, waiting for transfers between devices, shards(): lax.all_to_all(direction, 'dp', split_axis=1, concat_axis=0, tiled=True)  60.8 us
    all_to_all x1, waiting for transfers between devices, shards(): lax.all_to_all(regrouped, 'group', split_axis=0, concat_axis=0, tiled=True)  49.7 us
    all_to_all x1, starting transfers between devices, shards(): lax.all_to_all(direction, 'dp', split_axis=1, concat_axis=0, tiled=True)  19 us
    reshape x1, local copies, waits for them, and re-layouts, shards(): outgoing = outgoing.reshape(device_count, 1, row_count, col_count)  18.7 us
    dot_general x1, matrix products, shards(): jnp.einsum('sg,dgrw->sdrw', source_pick, pieces, preferred_element_type=j...  18.5 us
    dot_general x1, matrix products, shards(): jnp.einsum('sij,sjk->sik', left_part, right_root, preferred_element_type=...  17.7 us
  transfers between devices with their start and end apart: 4, of which 4 were waited for; matrix products, arithmetic and copies ran while one was open for 0% of the time, Pallas kernels for 0%

commit v1 on v0

v1 whole, which is shorter than its diff:
```python
import functools

import jax
import jax.numpy as jnp
from jax import lax
from jax.experimental import pallas as pl
from jax.experimental.pallas import tpu as pltpu
from jax.sharding import PartitionSpec as P

CAPG = 4
CHUNKS = 2
STRIP = 256


def move_kernel(count, index_ref, source_ref, out_ref, sems):
    copies = [
        pltpu.make_async_copy(source_ref.at[index_ref[i]], out_ref.at[i], sems.at[i])
        for i in range(count)
    ]
    for copy in copies:
        copy.start()
    for copy in copies:
        copy.wait()


def move(source, index):
    count = index.shape[0]
    size = source.size // source.shape[0] * source.dtype.itemsize
    return pl.pallas_call(
        functools.partial(move_kernel, count),
        out_shape=jax.ShapeDtypeStruct((count,) + source.shape[1:], source.dtype),
        in_specs=[
            pl.BlockSpec(memory_space=pltpu.SMEM),
            pl.BlockSpec(memory_space=pl.ANY),
        ],
        out_specs=pl.BlockSpec(memory_space=pl.ANY),
        scratch_shapes=[pltpu.SemaphoreType.DMA((count,))],
        cost_estimate=pl.CostEstimate(
            flops=0, bytes_accessed=2 * count * size, transcendentals=0
        ),
        name="move",
    )(index, source)


def cut_kernel(chunk, source_ref, out_ref, sems):
    copies = [
        pltpu.make_async_copy(source_ref.at[:, d, chunk], out_ref.at[d], sems.at[d])
        for d in range(out_ref.shape[0])
    ]
    for copy in copies:
        copy.start()
    for copy in copies:
        copy.wait()


def cut(partial, chunk):
    blocks, places, _, rows, cols = partial.shape
    return pl.pallas_call(
        functools.partial(cut_kernel, chunk),
        out_shape=jax.ShapeDtypeStruct((places, blocks, rows, cols), partial.dtype),
        in_specs=[pl.BlockSpec(memory_space=pl.ANY)],
        out_specs=pl.BlockSpec(memory_space=pl.ANY),
        scratch_shapes=[pltpu.SemaphoreType.DMA((places,))],
        cost_estimate=pl.CostEstimate(
            flops=0, bytes_accessed=4 * places * blocks * rows * cols, transcendentals=0
        ),
        name="cut",
    )(partial)


def precondition_kernel(chunks, left_ref, right_ref, *refs):
    grads, outs = refs[:chunks], refs[chunks : 2 * chunks]
    block, product = refs[2 * chunks :]
    size = block.shape[0]
    for c in range(chunks):
        piece = grads[c].shape[2]
        for d in range(grads[c].shape[0]):
            start = (d * chunks + c) * piece
            block[start : start + piece, :] = grads[c][d, 0]
    grad_sum = jnp.zeros((1, size), jnp.float32)
    prod_sum = jnp.zeros((1, size), jnp.float32)
    for i in range(size // STRIP):
        rows = slice(i * STRIP, (i + 1) * STRIP)
        left_part = jnp.dot(
            left_ref[0, rows, :], block[...], preferred_element_type=jnp.float32
        ).astype(jnp.bfloat16)
        strip = jnp.dot(left_part, right_ref[0], preferred_element_type=jnp.float32)
        product[rows, :] = strip
        prod_sum += jnp.sum(strip * strip, axis=0, keepdims=True)
        grad = block[rows, :].astype(jnp.float32)
        grad_sum += jnp.sum(grad * grad, axis=0, keepdims=True)
    scale = 1.0 / (size * size)
    grad_norm = jnp.sqrt(jnp.sum(grad_sum, axis=1, keepdims=True) * scale)
    prod_norm = jnp.sqrt(jnp.sum(prod_sum, axis=1, keepdims=True) * scale + 1e-06)
    ratio = grad_norm / prod_norm
    for c in range(chunks):
        piece = outs[c].shape[2]
        for d in range(outs[c].shape[0]):
            start = (d * chunks + c) * piece
            outs[c][d, 0] = (product[start : start + piece, :] * ratio).astype(jnp.bfloat16)


def precondition(left_root, right_root, pieces):
    slots, size, _ = left_root.shape
    chunks = len(pieces)
    root_spec = pl.BlockSpec((1, size, size), lambda s: (s, 0, 0))
    part = pieces[0].shape
    part_spec = pl.BlockSpec((part[0], 1) + part[2:], lambda s: (0, s, 0, 0))
    return pl.pallas_call(
        functools.partial(precondition_kernel, chunks),
        grid=(slots,),
        out_shape=[jax.ShapeDtypeStruct(part, jnp.bfloat16)] * chunks,
        in_specs=[root_spec, root_spec] + [part_spec] * chunks,
        out_specs=[part_spec] * chunks,
        scratch_shapes=[
            pltpu.VMEM((size, size), jnp.bfloat16),
            pltpu.VMEM((size, size), jnp.float32),
        ],
        compiler_params=pltpu.CompilerParams(vmem_limit_bytes=48 * 1024 * 1024),
        cost_estimate=pl.CostEstimate(
            flops=4 * slots * size**3, bytes_accessed=8 * slots * size * size, transcendentals=0
        ),
        name="precondition",
    )(left_root, right_root, *pieces)


def update_kernel(chunks, index_ref, momentum_ref, *refs):
    parts, out = refs[:chunks], refs[chunks]
    for c in range(chunks):
        piece = parts[c].shape[1]
        rows = slice(c * piece, (c + 1) * piece)
        out[0, rows, :] = 0.9 * momentum_ref[0, rows, :] + parts[c][0].astype(jnp.float32)


def update(momentum, parts, index):
    chunks = len(parts)
    count, rows, cols = momentum.shape
    own = pl.BlockSpec((1, rows, cols), lambda j, index: (j, 0, 0))
    part = pl.BlockSpec((1, rows // chunks, cols), lambda j, index: (index[j], 0, 0))
    return pl.pallas_call(
        functools.partial(update_kernel, chunks),
        out_shape=jax.ShapeDtypeStruct(momentum.shape, jnp.float32),
        grid_spec=pltpu.PrefetchScalarGridSpec(
            num_scalar_prefetch=1,
            grid=(count,),
            in_specs=[own] + [part] * chunks,
            out_specs=own,
        ),
        name="update",
    )(index, momentum, *parts)


def pick(match, values):
    return jnp.sum(jnp.where(match, values[None, :], 0), axis=1).astype(jnp.int32)


def shards(grad_partial, left_root, right_root, block_owner, momentum):
    dp_count = lax.axis_size("dp")
    group_count = lax.axis_size("group")
    group_index = lax.axis_index("group")
    slot_count, size, _ = left_root.shape
    local_count, row_count, col_count = momentum.shape
    block_ids = jnp.arange(block_owner.shape[0], dtype=jnp.int32)
    owner_device = block_owner // slot_count
    owner_group = owner_device % group_count
    owner_place = owner_device // group_count * slot_count + block_owner % slot_count
    source_group = block_ids // local_count
    earlier = (
        (block_ids[None, :] < block_ids[:, None])
        & (source_group[None, :] == source_group[:, None])
        & (owner_group[None, :] == owner_group[:, None])
    )
    rank_in = jnp.sum(earlier.astype(jnp.int32), axis=1)
    buffer_size = group_count * CAPG
    column = source_group * CAPG + rank_in
    target = lax.dynamic_slice_in_dim(
        owner_group * CAPG + rank_in, group_index * local_count, local_count
    )
    held_here = (owner_group == group_index)[None, :]
    columns = jnp.arange(buffer_size, dtype=jnp.int32)[:, None]
    places = jnp.arange(dp_count * slot_count, dtype=jnp.int32)[:, None]
    to_group = pick(target[None, :] == columns, jnp.arange(local_count, dtype=jnp.int32))
    to_owner = pick(held_here & (owner_place[None, :] == places), column)
    to_source = pick(held_here & (column[None, :] == columns), owner_place)

    piece = row_count // CHUNKS
    partial = grad_partial[0].reshape(local_count, dp_count, CHUNKS, piece, col_count)
    pieces = []
    for c in range(CHUNKS):
        rows = lax.psum_scatter(cut(partial, c), "dp", scatter_dimension=0, tiled=True)
        sent = move(rows.reshape(local_count, piece, col_count), to_group)
        sent = sent.reshape(group_count, CAPG * piece, col_count)
        came = lax.all_to_all(sent, "group", split_axis=0, concat_axis=0, tiled=True)
        sent = move(came.reshape(buffer_size, piece, col_count), to_owner)
        sent = sent.reshape(dp_count, slot_count * piece, col_count)
        came = lax.all_to_all(sent, "dp", split_axis=0, concat_axis=0, tiled=True)
        pieces.append(came.reshape(dp_count, slot_count, piece, col_count))
    directions = precondition(left_root, right_root, pieces)
    parts = []
    for c in range(CHUNKS):
        sent = directions[c].reshape(dp_count, slot_count * piece, col_count)
        came = lax.all_to_all(sent, "dp", split_axis=0, concat_axis=0, tiled=True)
        sent = move(came.reshape(dp_count * slot_count, piece, col_count), to_source)
        sent = sent.reshape(group_count, CAPG * piece, col_count)
        came = lax.all_to_all(sent, "group", split_axis=0, concat_axis=0, tiled=True)
        parts.append(came.reshape(buffer_size, piece, col_count))
    return update(momentum, parts, target)


def solution(mesh):
    return jax.shard_map(
        shards,
        mesh=mesh,
        in_specs=(
            P("dp", "group", None, None),
            P(("dp", "group"), None, None),
            P(("dp", "group"), None, None),
            P(),
            P("group", "dp", None),
        ),
        out_specs=P("group", "dp", None),
        check_vma=False,
    )
```

time: 632 us -> 1010 us (1.60); the launches traced: 623 us -> 1010 us
  Pallas kernels: 0 us -> 860 us
  waiting for transfers between devices: 445 us -> 14.1 us
  blocking collectives: 0 us -> 98.9 us
  local copies, waits for them, and re-layouts: 67.7 us -> 3.4 us
  matrix products: 56.4 us -> 0 us
  starting transfers between devices: 32.4 us -> 21.8 us
    pallas_call x0 -> x10, Pallas kernels: none -> 860 us  [the longest x2 447 us: cut(): pl.pallas_call(functools.partial(cut_kernel, chunk), out_shape=jax.ShapeD...]
    all_to_all x3 -> x5, waiting for transfers between devices: 337 us -> 0.01 us  [the longest x3 0.01 us: shards(): lax.all_to_all(sent, 'group', split_axis=0, concat_axis=0, tiled=True)]
    reduce_scatter x1 -> x0, waiting for transfers between devices: 108 us -> none  [shards(): lax.psum_scatter(grad_partial, 'dp', scatter_dimension=2, tiled=True)]
    all_to_all x0 -> x3, blocking collectives: none -> 98.9 us  [the longest x2 66.6 us: shards(): came = lax.all_to_all(sent, 'dp', split_axis=0, concat_axis=0, tiled=True)]
    dot_general x5 -> x0, matrix products: 56.4 us -> none  [the longest x1 18.5 us: shards(): jnp.einsum('sg,dgrw->sdrw', source_pick, pieces, preferred_element_type=j...]
    reshape x4 -> x0, local copies, waits for them, and re-layouts: 38.6 us -> none  [the longest x1 18.7 us: shards(): outgoing = outgoing.reshape(device_count, 1, row_count, col_count)]
    all_to_all x3 -> x0, local copies, waits for them, and re-layouts: 22.6 us -> none  [the longest x2 15.9 us: shards(): lax.all_to_all(direction, 'dp', split_axis=1, concat_axis=0, tiled=True)]
    unnamed x1 -> x4, waiting for transfers between devices: 0.71 us -> 14.1 us
  transfers between devices with their start and end apart: 4 -> 7, of which waited for: 4 -> 1; matrix products, arithmetic and copies ran while one was open for 0% -> 0% of each run, Pallas kernels for 0% -> 61%
where the time goes in v1:
time: 1010 us
  Pallas kernels  860 us (85%)
  blocking collectives  98.9 us (10%)
  starting transfers between devices  21.8 us (2%)
  waiting for transfers between devices  14.1 us (1%)
  between operations  13.6 us (1%)
    pallas_call x2, Pallas kernels, cut(): pl.pallas_call(functools.partial(cut_kernel, chunk), out_shape=jax.ShapeD...  447 us
    pallas_call x6, Pallas kernels, move(): pl.pallas_call(functools.partial(move_kernel, count), out_shape=jax.Shape...  394 us
    all_to_all x2, blocking collectives, shards(): came = lax.all_to_all(sent, 'dp', split_axis=0, concat_axis=0, tiled=True)  66.6 us
    all_to_all x1, blocking collectives, shards(): lax.all_to_all(sent, 'group', split_axis=0, concat_axis=0, tiled=True)  32.3 us
  transfers between devices with their start and end apart: 7, of which 1 were waited for; matrix products, arithmetic and copies ran while one was open for 0% of the time, Pallas kernels for 61%

profile of v1, /device:TPU:0, one launch (start us, length us, event | category | flops | bytes accessed | tf_op | source)
XLA Modules:
  0.0 1013.6 jit_solution(15976090520059603641)
XLA Ops:
  6.5 223.6 %cut.3 = bf16[16,7,32,1024]{3,2,1,0:T(8,128)(2,1)} custom-call(bf16[7,16,2,32,1024]{4,3,2,1,0:T(8,128)(2,1)} %bitcast.21), custom_call_target="tpu_custom_call" | custom-call | bytes 14680064 | tf_op jit(solution)/shard_map/cut/pallas_call | solution.py:58
  230.1 0.0 reduce-scatter.9.cloned.1.call-update
  230.2 0.0 reduce-scatter.7.cloned.1.call-start
  230.2 223.6 %cut.2 = bf16[16,7,32,1024]{3,2,1,0:T(8,128)(2,1)} custom-call(bf16[7,16,2,32,1024]{4,3,2,1,0:T(8,128)(2,1)} %bitcast.22), custom_call_target="tpu_custom_call" | custom-call | bytes 14680064 | tf_op jit(solution)/shard_map/cut/pallas_call | solution.py:58
  453.8 0.0 copy-start.3
  453.8 0.0 reduce-scatter.7.cloned.1.call-update
  453.9 0.6 copy-done.3
  454.5 0.2 convert_reduce_fusion
  454.7 0.1 dynamic_slice.3.index_ref
  454.8 0.6 select_reduce_fusion.2.index_ref
  455.4 65.6 %move.8 = bf16[32,32,1024]{2,1,0:T(8,128)(2,1)} custom-call(s32[32]{0:T(128)} %select_reduce_fusion.2.index_ref, bf16[7,32,1024]{2,1,0:T(8,128)(2,1)} %bitcast.35), custom_call_target="tpu_custom_call" | custom-call | bytes 4194304 | tf_op jit(solution)/shard_map/move/pallas_call | solution.py:29
  521.0 4.4 all-to-all-start.2
  525.4 14.1 %reduce-scatter.7.cloned.1.call-done = bf16[1,7,32,1024]{3,2,1,0:T(8,128)(2,1)} async-done(((bf16[16,7,32,1024]{3,2,1,0:T(8,128)(2,1)}), bf16[1,7,32,1024]{3,2,1,0:T(8,128)(2,1)}) %reduce-scatter.7.cloned.1.call-update) | async-done | bytes 458768
  539.4 65.6 %move.6 = bf16[32,32,1024]{2,1,0:T(8,128)(2,1)} custom-call(s32[32]{0:T(128)} %select_reduce_fusion.2.index_ref, bf16[7,32,1024]{2,1,0:T(8,128)(2,1)} %bitcast.36), custom_call_target="tpu_custom_call" | custom-call | bytes 4194304 | tf_op jit(solution)/shard_map/move/pallas_call | solution.py:29
  605.1 1.4 copy-done
  606.4 4.3 all-to-all-start
  610.8 0.7 select_reduce_fusion
  611.5 65.6 %move.9 = bf16[32,32,1024]{2,1,0:T(8,128)(2,1)} custom-call(s32[32]{0:T(128)} %get-tuple-element.9.index_ref, bf16[32,32,1024]{2,1,0:T(8,128)(2,1)} %bitcast.23), custom_call_target="tpu_custom_call" | custom-call | bytes 4194304 | tf_op jit(solution)/shard_map/move/pallas_call | solution.py:29
  677.1 0.0 all-to-all-done
  677.1 4.9 all-to-all-start.3
  682.0 65.6 %move.7 = bf16[32,32,1024]{2,1,0:T(8,128)(2,1)} custom-call(s32[32]{0:T(128)} %get-tuple-element.9.index_ref, bf16[32,32,1024]{2,1,0:T(8,128)(2,1)} %bitcast.4.source_ref), custom_call_target="tpu_custom_call" | custom-call | bytes 4194304 | tf_op jit(solution)/shard_map/move/pallas_call | solution.py:29
  747.6 0.0 all-to-all-done.3
  747.6 35.6 %all_to_all.40 = bf16[16,64,1024]{2,1,0:T(8,128)(2,1)} all-to-all(bf16[16,64,1024]{2,1,0:T(8,128)(2,1)} %bitcast.30), channel_id=1, replica_groups=mesh['dp'=16,'group'=8] {'dp'}, dimensions={0} | all-to-all | bytes 4194304 | tf_op jit(solution)/shard_map/all_to_all | solution.py:196
  783.3 13.6 %precondition.1 = (bf16[16,2,32,1024]{3,2,1,0:T(8,128)(2,1)}, bf16[16,2,32,1024]{3,2,1,0:T(8,128)(2,1)S(1)}) custom-call(bf16[2,1024,1024]{2,1,0:T(8,128)(2,1)} %left_ref.1, bf16[2,1024,1024]{2,1,0:T(8,128)(2,1)} %right_ref.1, bf16[16,2,32,1024]{3,2,1,0:T(8,128)(2,1)} %bitcast.34, bf16[16,2,32,1024]{3,2,1,0:T(8,128)(2,1)} %bitcast.33), custom_call_target="tpu_custom_call" | custom-call | flops 8589934592 | bytes 16777216 | tf_op jit(solution)/shard_map/precondition/pallas_call | solution.py:109
  796.9 31.0 %all_to_all.41 = bf16[16,64,1024]{2,1,0:T(8,128)(2,1)} all-to-all(bf16[16,64,1024]{2,1,0:T(8,128)(2,1)S(1)} %bitcast.20), channel_id=1, replica_groups=mesh['dp'=16,'group'=8] {'dp'}, dimensions={0} | all-to-all | bytes 4194304 | tf_op jit(solution)/shard_map/all_to_all | solution.py:202
  827.8 3.7 all-to-all-start.4
  831.6 65.6 %move.11 = bf16[32,32,1024]{2,1,0:T(8,128)(2,1)} custom-call(s32[32]{0:T(128)} %get-tuple-element.10.index_ref, bf16[32,32,1024]{2,1,0:T(8,128)(2,1)} %bitcast.29), custom_call_target="tpu_custom_call" | custom-call | bytes 4194304 | tf_op jit(solution)/shard_map/move/pallas_call | solution.py:29
  897.2 1.4 copy-done.1
  898.5 4.3 all-to-all-start.7
  902.9 65.6 %move.10 = bf16[32,32,1024]{2,1,0:T(8,128)(2,1)} custom-call(s32[32]{0:T(128)} %get-tuple-element.10.index_ref, bf16[32,32,1024]{2,1,0:T(8,128)(2,1)} %bitcast.25), custom_call_target="tpu_custom_call" | custom-call | bytes 4194304 | tf_op jit(solution)/shard_map/move/pallas_call | solution.py:29
  968.5 32.3 %all_to_all.42 = bf16[8,128,1024]{2,1,0:T(8,128)(2,1)} all-to-all(bf16[8,128,1024]{2,1,0:T(8,128)(2,1)} %bitcast.31), channel_id=1, replica_groups=mesh['dp'=16,'group'=8] {'group'}, dimensions={0} | all-to-all | bytes 4194304 | tf_op jit(solution)/shard_map/all_to_all | solution.py:205
  1000.8 5.9 update.1
  (14 shorter events, 0.1 us)
Async XLA Ops:
  6.5 448.8 %reduce-scatter.9.cloned.1.call-start = ((), (), s32[]{:S(2)}) async-start(), calls=%async_computation.11 | async-start | bytes 7798784
  230.2 309.3 %reduce-scatter.7.cloned.1.call-start = ((), (), s32[]{:S(2)}) async-start(), calls=%async_computation.10 | async-start | bytes 7798784
  453.8 0.7 copy-start.3
  454.8 66.2 %copy-start.4 = (s32[7]{0:T(128)}, s32[7]{0:T(128)S(1)}, u32[]{:S(2)}) copy-start(s32[7]{0:T(128)S(1)} %dynamic_slice.3.index_ref) | copy-start | bytes 88
  521.0 84.1 %all-to-all-start.2 = ((bf16[8,128,1024]{2,1,0:T(8,128)(2,1)}), bf16[8,128,1024]{2,1,0:T(8,128)(2,1)S(1)}, u32[]{:S(2)}, u32[]{:S(2)}) async-start(bf16[8,128,1024]{2,1,0:T(8,128)(2,1)} %bitcast.28), calls=%async_computation.2 | async-start | bytes 4194304 | tf_op jit(solution)/shard_map/all_to_all | solution.py:193
  605.0 1.4 copy-start
  606.4 70.6 %all-to-all-start = ((bf16[8,128,1024]{2,1,0:T(8,128)(2,1)}), bf16[8,128,1024]{2,1,0:T(8,128)(2,1)}, u32[]{:S(2)}, u32[]{:S(2)}) async-start(bf16[8,128,1024]{2,1,0:T(8,128)(2,1)} %bitcast.24), calls=%async_computation | async-start | bytes 4194304 | tf_op jit(solution)/shard_map/all_to_all | solution.py:193
  677.1 70.6 %all-to-all-start.3 = ((bf16[16,64,1024]{2,1,0:T(8,128)(2,1)}), bf16[16,64,1024]{2,1,0:T(8,128)(2,1)S(1)}, u32[]{:S(2)}, u32[]{:S(2)}) async-start(bf16[16,64,1024]{2,1,0:T(8,128)(2,1)} %bitcast.26), calls=%async_computation.3 | async-start | bytes 4194304 | tf_op jit(solution)/shard_map/all_to_all | solution.py:196
  747.6 35.6 %copy-start.2 = (bf16[16,64,1024]{2,1,0:T(8,128)(2,1)}, bf16[16,64,1024]{2,1,0:T(8,128)(2,1)S(1)}, u32[]{:S(2)}) copy-start(bf16[16,64,1024]{2,1,0:T(8,128)(2,1)S(1)} %all-to-all-done.3) | copy-start | bytes 6291460
  827.8 69.3 %all-to-all-start.4 = ((bf16[16,64,1024]{2,1,0:T(8,128)(2,1)}), bf16[16,64,1024]{2,1,0:T(8,128)(2,1)S(1)}, u32[]{:S(2)}, u32[]{:S(2)}) async-start(bf16[16,64,1024]{2,1,0:T(8,128)(2,1)} %bitcast.12), calls=%async_computation.4 | async-start | bytes 4194304 | tf_op jit(solution)/shard_map/all_to_all | solution.py:202
  897.2 1.4 copy-start.1
  898.5 70.0 %all-to-all-start.7 = ((bf16[8,128,1024]{2,1,0:T(8,128)(2,1)}), bf16[8,128,1024]{2,1,0:T(8,128)(2,1)}, u32[]{:S(2)}, u32[]{:S(2)}) async-start(bf16[8,128,1024]{2,1,0:T(8,128)(2,1)} %bitcast.27), calls=%async_computation.7 | async-start | bytes 4194304 | tf_op jit(solution)/shard_map/all_to_all | solution.py:205
Sparse Core Ops, SparseCore 0:
  230.3 85.4 reduce-scatter.8
  454.0 85.4 reduce-scatter.6

commit v2 on v1

--- a/solution.py
+++ b/solution.py
@@ -10,17 +10,42 @@
 CAPG = 4
 CHUNKS = 2
 STRIP = 256
-
-
-def move_kernel(count, index_ref, source_ref, out_ref, sems):
-    copies = [
-        pltpu.make_async_copy(source_ref.at[index_ref[i]], out_ref.at[i], sems.at[i])
-        for i in range(count)
+VMEM_LIMIT = 48 * 1024 * 1024
+
+
+def stage(sources, targets, buffer, loads, stores):
+    count = len(sources)
+    first = [
+        pltpu.make_async_copy(sources[i], buffer.at[i], loads.at[i]) for i in range(count)
     ]
-    for copy in copies:
+    second = [
+        pltpu.make_async_copy(buffer.at[i], targets[i], stores.at[i]) for i in range(count)
+    ]
+    for copy in first:
         copy.start()
-    for copy in copies:
+    for i in range(count):
+        first[i].wait()
+        second[i].start()
+    for copy in second:
         copy.wait()
+
+
+def staging(count, shape, dtype):
+    return [
+        pltpu.VMEM((count,) + shape, dtype),
+        pltpu.SemaphoreType.DMA((count,)),
+        pltpu.SemaphoreType.DMA((count,)),
+    ]
+
+
+def move_kernel(count, index_ref, source_ref, out_ref, buffer, loads, stores):
+    stage(
+        [source_ref.at[index_ref[i]] for i in range(count)],
+        [out_ref.at[i] for i in range(count)],
+        buffer,
+        loads,
+        stores,
+    )
 
 
 def move(source, index):
@@ -34,7 +59,8 @@
             pl.BlockSpec(memory_space=pl.ANY),
         ],
         out_specs=pl.BlockSpec(memory_space=pl.ANY),
-        scratch_shapes=[pltpu.SemaphoreType.DMA((count,))],
+        scratch_shapes=staging(count, source.shape[1:], source.dtype),
+        compiler_params=pltpu.CompilerParams(vmem_limit_bytes=VMEM_LIMIT),
         cost_estimate=pl.CostEstimate(
             flops=0, bytes_accessed=2 * count * size, transcendentals=0
         ),
@@ -42,15 +68,15 @@
     )(index, source)
 
 
-def cut_kernel(chunk, source_ref, out_ref, sems):
-    copies = [
-        pltpu.make_async_copy(source_ref.at[:, d, chunk], out_ref.at[d], sems.at[d])
-        for d in range(out_ref.shape[0])
-    ]
-    for copy in copies:
-        copy.start()
-    for copy in copies:
-        copy.wait()
+def cut_kernel(chunk, source_ref, out_ref, buffer, loads, stores):
+    places = out_ref.shape[0]
+    stage(
+        [source_ref.at[:, d, chunk] for d in range(places)],
+        [out_ref.at[d] for d in range(places)],
+        buffer,
+        loads,
+        stores,
+    )
 
 
 def cut(partial, chunk):
@@ -60,7 +86,8 @@
         out_shape=jax.ShapeDtypeStruct((places, blocks, rows, cols), partial.dtype),
         in_specs=[pl.BlockSpec(memory_space=pl.ANY)],
         out_specs=pl.BlockSpec(memory_space=pl.ANY),
-        scratch_shapes=[pltpu.SemaphoreType.DMA((places,))],
+        scratch_shapes=staging(places, (blocks, rows, cols), partial.dtype),
+        compiler_params=pltpu.CompilerParams(vmem_limit_bytes=VMEM_LIMIT),
         cost_estimate=pl.CostEstimate(
             flops=0, bytes_accessed=4 * places * blocks * rows * cols, transcendentals=0
         ),
@@ -116,7 +143,7 @@
             pltpu.VMEM((size, size), jnp.bfloat16),
             pltpu.VMEM((size, size), jnp.float32),
         ],
-        compiler_params=pltpu.CompilerParams(vmem_limit_bytes=48 * 1024 * 1024),
+        compiler_params=pltpu.CompilerParams(vmem_limit_bytes=VMEM_LIMIT),
         cost_estimate=pl.CostEstimate(
             flops=4 * slots * size**3, bytes_accessed=8 * slots * size * size, transcendentals=0
         ),

time: 1010 us -> 438 us (0.43)
  Pallas kernels: 860 us -> 71.8 us
  waiting for transfers between devices: 14.1 us -> 228 us
    pallas_call x2, Pallas kernels: 447 us -> 11.9 us  [cut(): pl.pallas_call(functools.partial(cut_kernel, chunk), out_shape=jax.ShapeD...]
    pallas_call x6, Pallas kernels: 394 us -> 41.1 us  [move(): pl.pallas_call(functools.partial(move_kernel, count), out_shape=jax.Shape...]
    unnamed x4, waiting for transfers between devices: 14.1 us -> 151 us
    all_to_all x2, waiting for transfers between devices: 0.01 us -> 39.8 us  [shards(): came = lax.all_to_all(sent, 'dp', split_axis=0, concat_axis=0, tiled=True)]
    all_to_all x3, waiting for transfers between devices: 0.01 us -> 37.1 us  [shards(): lax.all_to_all(sent, 'group', split_axis=0, concat_axis=0, tiled=True)]
  transfers between devices with their start and end apart: 7 -> 7, of which waited for: 1 -> 6; matrix products, arithmetic and copies ran while one was open for 0% -> 0% of each run, Pallas kernels for 61% -> 11%
where the time goes in v2:
time: 438 us; the launch traced here: 436 us
  waiting for transfers between devices  228 us (52%)
  blocking collectives  89.9 us (21%)
  Pallas kernels  71.8 us (16%)
  starting transfers between devices  21.7 us (5%)
  between operations  13.6 us (3%)
  local copies, waits for them, and re-layouts  11 us (3%)
    unnamed x4, waiting for transfers between devices  151 us
    all_to_all x2, blocking collectives, shards(): came = lax.all_to_all(sent, 'dp', split_axis=0, concat_axis=0, tiled=True)  58 us
    pallas_call x6, Pallas kernels, move(): pl.pallas_call(functools.partial(move_kernel, count), out_shape=jax.Shape...  41.1 us
    all_to_all x2, waiting for transfers between devices, shards(): came = lax.all_to_all(sent, 'dp', split_axis=0, concat_axis=0, tiled=True)  39.8 us
    all_to_all x3, waiting for transfers between devices, shards(): lax.all_to_all(sent, 'group', split_axis=0, concat_axis=0, tiled=True)  37.1 us
    all_to_all x1, blocking collectives, shards(): lax.all_to_all(sent, 'group', split_axis=0, concat_axis=0, tiled=True)  31.8 us
    all_to_all x3, starting transfers between devices, shards(): lax.all_to_all(sent, 'group', split_axis=0, concat_axis=0, tiled=True)  12.9 us
    pallas_call x1, Pallas kernels, precondition(): pl.pallas_call(functools.partial(precondition_kernel, chunks), grid=(slot...  12.8 us
  transfers between devices with their start and end apart: 7, of which 6 were waited for; matrix products, arithmetic and copies ran while one was open for 0% of the time, Pallas kernels for 11%

profile of v2, /device:TPU:0, one launch (start us, length us, event | category | flops | bytes accessed | tf_op | source)
XLA Modules:
  0.0 436.4 jit_solution(6116623877222390578)
XLA Ops:
  6.5 5.9 %cut.3 = bf16[16,7,32,1024]{3,2,1,0:T(8,128)(2,1)} custom-call(bf16[7,16,2,32,1024]{4,3,2,1,0:T(8,128)(2,1)} %bitcast.33), custom_call_target="tpu_custom_call" | custom-call | bytes 14680064 | tf_op jit(solution)/shard_map/cut/pallas_call | solution.py:84
  12.6 6.0 %cut.2 = bf16[16,7,32,1024]{3,2,1,0:T(8,128)(2,1)} custom-call(bf16[7,16,2,32,1024]{4,3,2,1,0:T(8,128)(2,1)} %bitcast.34), custom_call_target="tpu_custom_call" | custom-call | bytes 14680064 | tf_op jit(solution)/shard_map/cut/pallas_call | solution.py:84
  19.6 78.6 %reduce-scatter.9.cloned.1.call-done = bf16[1,7,32,1024]{3,2,1,0:T(8,128)(2,1)} async-done(((bf16[16,7,32,1024]{3,2,1,0:T(8,128)(2,1)}), bf16[1,7,32,1024]{3,2,1,0:T(8,128)(2,1)}) %reduce-scatter.9.cloned.1.call-update) | async-done | bytes 458768
  98.2 1.0 copy-done.7
  99.2 7.3 %move.8 = bf16[32,32,1024]{2,1,0:T(8,128)(2,1)S(1)} custom-call(s32[32]{0:T(128)S(1)} %select_reduce_fusion.2.index_ref, bf16[7,32,1024]{2,1,0:T(8,128)(2,1)S(1)} %bitcast.31), custom_call_target="tpu_custom_call" | custom-call | bytes 4194304 | tf_op jit(solution)/shard_map/move/pallas_call | solution.py:54
  106.5 1.4 copy-done.3
  107.9 4.2 all-to-all-start.2
  112.1 72.6 %reduce-scatter.7.cloned.1.call-done = bf16[1,7,32,1024]{3,2,1,0:T(8,128)(2,1)} async-done(((bf16[16,7,32,1024]{3,2,1,0:T(8,128)(2,1)}), bf16[1,7,32,1024]{3,2,1,0:T(8,128)(2,1)}) %reduce-scatter.7.cloned.1.call-update) | async-done | bytes 458768
  184.7 1.0 copy-done.8
  185.7 7.3 %move.6 = bf16[32,32,1024]{2,1,0:T(8,128)(2,1)S(1)} custom-call(s32[32]{0:T(128)S(1)} %select_reduce_fusion.2.index_ref, bf16[7,32,1024]{2,1,0:T(8,128)(2,1)S(1)} %bitcast.32), custom_call_target="tpu_custom_call" | custom-call | bytes 4194304 | tf_op jit(solution)/shard_map/move/pallas_call | solution.py:54
  193.0 1.3 copy-done
  194.3 4.3 all-to-all-start
  198.7 7.3 %move.9 = bf16[32,32,1024]{2,1,0:T(8,128)(2,1)S(1)} custom-call(s32[32]{0:T(128)S(1)} %get-tuple-element.9.index_ref, bf16[32,32,1024]{2,1,0:T(8,128)(2,1)S(1)} %bitcast.20), custom_call_target="tpu_custom_call" | custom-call | bytes 4194304 | tf_op jit(solution)/shard_map/move/pallas_call | solution.py:54
  206.1 1.3 copy-done.1
  207.4 18.5 %all-to-all-done = bf16[8,128,1024]{2,1,0:T(8,128)(2,1)} async-done(((bf16[8,128,1024]{2,1,0:T(8,128)(2,1)}), bf16[8,128,1024]{2,1,0:T(8,128)(2,1)}, u32[]{:S(2)}, u32[]{:S(2)}) %all-to-all-start) | async-done | bytes 2097184 | tf_op jit(solution)/shard_map/all_to_all | solution.py:220
  225.9 5.0 %all-to-all-start.3 = ((bf16[16,64,1024]{2,1,0:T(8,128)(2,1)}), bf16[16,64,1024]{2,1,0:T(8,128)(2,1)}, u32[]{:S(2)}, u32[]{:S(2)}) async-start(bf16[16,64,1024]{2,1,0:T(8,128)(2,1)} %bitcast.23), calls=%async_computation.3 | async-start | bytes 4194304 | tf_op jit(solution)/shard_map/all_to_all | solution.py:223
  230.9 4.7 %move.7 = bf16[32,32,1024]{2,1,0:T(8,128)(2,1)S(1)} custom-call(s32[32]{0:T(128)S(1)} %get-tuple-element.9.index_ref, bf16[32,32,1024]{2,1,0:T(8,128)(2,1)} %bitcast.4.source_ref), custom_call_target="tpu_custom_call" | custom-call | bytes 4194304 | tf_op jit(solution)/shard_map/move/pallas_call | solution.py:54
  235.6 25.3 %all-to-all-done.3 = bf16[16,64,1024]{2,1,0:T(8,128)(2,1)} async-done(((bf16[16,64,1024]{2,1,0:T(8,128)(2,1)}), bf16[16,64,1024]{2,1,0:T(8,128)(2,1)}, u32[]{:S(2)}, u32[]{:S(2)}) %all-to-all-start.3) | async-done | bytes 2097184 | tf_op jit(solution)/shard_map/all_to_all | solution.py:223
  261.0 29.8 %all_to_all.40 = bf16[16,64,1024]{2,1,0:T(8,128)(2,1)} all-to-all(bf16[16,64,1024]{2,1,0:T(8,128)(2,1)S(1)} %bitcast.27), channel_id=1, replica_groups=mesh['dp'=16,'group'=8] {'dp'}, dimensions={0} | all-to-all | bytes 4194304 | tf_op jit(solution)/shard_map/all_to_all | solution.py:223
  290.7 12.8 %precondition.1 = (bf16[16,2,32,1024]{3,2,1,0:T(8,128)(2,1)S(1)}, bf16[16,2,32,1024]{3,2,1,0:T(8,128)(2,1)S(1)}) custom-call(bf16[2,1024,1024]{2,1,0:T(8,128)(2,1)} %left_ref.1, bf16[2,1024,1024]{2,1,0:T(8,128)(2,1)} %right_ref.1, bf16[16,2,32,1024]{3,2,1,0:T(8,128)(2,1)} %bitcast.36, bf16[16,2,32,1024]{3,2,1,0:T(8,128)(2,1)} %bitcast.11.refs_1_), custom_call_target="tpu_custom_call" | custom-call | flops 8589934592 | bytes 16777216 | tf_op jit(solution)/shard_map/precondition/pallas_call | solution.py:136
  303.6 28.2 %all_to_all.41 = bf16[16,64,1024]{2,1,0:T(8,128)(2,1)} all-to-all(bf16[16,64,1024]{2,1,0:T(8,128)(2,1)S(1)} %bitcast.30), channel_id=1, replica_groups=mesh['dp'=16,'group'=8] {'dp'}, dimensions={0} | all-to-all | bytes 4194304 | tf_op jit(solution)/shard_map/all_to_all | solution.py:229
  331.8 3.7 all-to-all-start.4
  335.6 1.6 copy-done.4
  337.1 7.3 %move.11 = bf16[32,32,1024]{2,1,0:T(8,128)(2,1)S(1)} custom-call(s32[32]{0:T(128)S(1)} %get-tuple-element.10.index_ref, bf16[32,32,1024]{2,1,0:T(8,128)(2,1)S(1)} %bitcast.26), custom_call_target="tpu_custom_call" | custom-call | bytes 4194304 | tf_op jit(solution)/shard_map/move/pallas_call | solution.py:54
  344.4 1.3 copy-done.2
  345.7 14.5 %all-to-all-done.4 = bf16[16,64,1024]{2,1,0:T(8,128)(2,1)S(1)} async-done(((bf16[16,64,1024]{2,1,0:T(8,128)(2,1)}), bf16[16,64,1024]{2,1,0:T(8,128)(2,1)S(1)}, u32[]{:S(2)}, u32[]{:S(2)}) %all-to-all-start.4) | async-done | bytes 2097184 | tf_op jit(solution)/shard_map/all_to_all | solution.py:229
  360.2 4.3 all-to-all-start.7
  364.6 7.3 %move.10 = bf16[32,32,1024]{2,1,0:T(8,128)(2,1)S(1)} custom-call(s32[32]{0:T(128)S(1)} %get-tuple-element.10.index_ref, bf16[32,32,1024]{2,1,0:T(8,128)(2,1)S(1)} %bitcast.22), custom_call_target="tpu_custom_call" | custom-call | bytes 4194304 | tf_op jit(solution)/shard_map/move/pallas_call | solution.py:54
  371.9 1.3 copy-done.5
  373.2 18.6 %all-to-all-done.7 = bf16[8,128,1024]{2,1,0:T(8,128)(2,1)} async-done(((bf16[8,128,1024]{2,1,0:T(8,128)(2,1)}), bf16[8,128,1024]{2,1,0:T(8,128)(2,1)}, u32[]{:S(2)}, u32[]{:S(2)}) %all-to-all-start.7) | async-done | bytes 2097184 | tf_op jit(solution)/shard_map/all_to_all | solution.py:232
  391.8 31.8 %all_to_all.42 = bf16[8,128,1024]{2,1,0:T(8,128)(2,1)} all-to-all(bf16[8,128,1024]{2,1,0:T(8,128)(2,1)} %bitcast.28), channel_id=1, replica_groups=mesh['dp'=16,'group'=8] {'group'}, dimensions={0} | all-to-all | bytes 4194304 | tf_op jit(solution)/shard_map/all_to_all | solution.py:232
  423.6 5.9 %update.1 = f32[7,64,1024]{2,1,0:T(8,128)} custom-call(s32[7]{0:T(128)} %copy-done.10, f32[7,64,1024]{2,1,0:T(8,128)} %momentum_ref.1, bf16[32,32,1024]{2,1,0:T(8,128)(2,1)} %bitcast.35, bf16[32,32,1024]{2,1,0:T(8,128)(2,1)} %bitcast.19.refs_1_), custom_call_target="tpu_custom_call" | custom-call | tf_op jit(solution)/shard_map/update/pallas_call | solution.py:167
  (26 shorter events, 1.2 us)
Async XLA Ops:
  6.5 91.6 %reduce-scatter.9.cloned.1.call-start = ((), (), s32[]{:S(2)}) async-start(), calls=%async_computation.11 | async-start | bytes 7798784
  12.5 172.1 %reduce-scatter.7.cloned.1.call-start = ((), (), s32[]{:S(2)}) async-start(), calls=%async_computation.10 | async-start | bytes 7798784
  18.5 0.7 copy-start.9
  19.5 88.4 %copy-start.10 = (s32[7]{0:T(128)}, s32[7]{0:T(128)S(1)}, u32[]{:S(2)}) copy-start(s32[7]{0:T(128)S(1)} %dynamic_slice.3.index_ref) | copy-start | bytes 88
  98.2 1.0 copy-start.7
  106.5 1.4 copy-start.3
  107.9 86.4 %all-to-all-start.2 = ((bf16[8,128,1024]{2,1,0:T(8,128)(2,1)}), bf16[8,128,1024]{2,1,0:T(8,128)(2,1)S(1)}, u32[]{:S(2)}, u32[]{:S(2)}) async-start(bf16[8,128,1024]{2,1,0:T(8,128)(2,1)} %bitcast.25), calls=%async_computation.2 | async-start | bytes 4194304 | tf_op jit(solution)/shard_map/all_to_all | solution.py:220
  184.7 1.0 copy-start.8
  193.0 1.3 copy-start
  194.3 31.6 %all-to-all-start = ((bf16[8,128,1024]{2,1,0:T(8,128)(2,1)}), bf16[8,128,1024]{2,1,0:T(8,128)(2,1)}, u32[]{:S(2)}, u32[]{:S(2)}) async-start(bf16[8,128,1024]{2,1,0:T(8,128)(2,1)} %bitcast.21), calls=%async_computation | async-start | bytes 4194304 | tf_op jit(solution)/shard_map/all_to_all | solution.py:220
  206.0 1.3 copy-start.1
  225.9 35.1 %all-to-all-start.3 = ((bf16[16,64,1024]{2,1,0:T(8,128)(2,1)}), bf16[16,64,1024]{2,1,0:T(8,128)(2,1)}, u32[]{:S(2)}, u32[]{:S(2)}) async-start(bf16[16,64,1024]{2,1,0:T(8,128)(2,1)} %bitcast.23), calls=%async_computation.3 | async-start | bytes 4194304 | tf_op jit(solution)/shard_map/all_to_all | solution.py:223
  303.6 28.2 %copy-start.6 = (bf16[16,2,32,1024]{3,2,1,0:T(8,128)(2,1)}, bf16[16,2,32,1024]{3,2,1,0:T(8,128)(2,1)S(1)}, u32[]{:S(2)}) copy-start(bf16[16,2,32,1024]{3,2,1,0:T(8,128)(2,1)S(1)} %get-tuple-element.7) | copy-start | bytes 6291460
  331.8 28.4 %all-to-all-start.4 = ((bf16[16,64,1024]{2,1,0:T(8,128)(2,1)}), bf16[16,64,1024]{2,1,0:T(8,128)(2,1)S(1)}, u32[]{:S(2)}, u32[]{:S(2)}) async-start(bf16[16,64,1024]{2,1,0:T(8,128)(2,1)} %bitcast.29), calls=%async_computation.4 | async-start | bytes 4194304 | tf_op jit(solution)/shard_map/all_to_all | solution.py:229
  335.5 1.6 copy-start.4
  344.4 1.3 copy-start.2
  360.2 31.5 %all-to-all-start.7 = ((bf16[8,128,1024]{2,1,0:T(8,128)(2,1)}), bf16[8,128,1024]{2,1,0:T(8,128)(2,1)}, u32[]{:S(2)}, u32[]{:S(2)}) async-start(bf16[8,128,1024]{2,1,0:T(8,128)(2,1)} %bitcast.24), calls=%async_computation.7 | async-start | bytes 4194304 | tf_op jit(solution)/shard_map/all_to_all | solution.py:232
  371.9 1.3 copy-start.5
Sparse Core Ops, SparseCore 0:
  12.6 85.4 reduce-scatter.8
  102.0 82.5 reduce-scatter.6

commit v3 on v2

v3 whole, which is shorter than its diff:
```python
import functools

import jax
import jax.numpy as jnp
from jax import lax
from jax.experimental import pallas as pl
from jax.experimental.pallas import tpu as pltpu
from jax.sharding import PartitionSpec as P

CAP = 5
CHUNKS = 1
STRIP = 256
VMEM_LIMIT = 48 * 1024 * 1024


def stage(copies, buffer, loads, stores):
    def load(i):
        return pltpu.make_async_copy(copies[i][1], buffer.at[i], loads.at[i])

    def store(i):
        return pltpu.make_async_copy(buffer.at[i], copies[i][2], stores.at[i])

    for i, (valid, _, _) in enumerate(copies):

        @pl.when(valid)
        def _(i=i):
            load(i).start()

    for i, (valid, _, _) in enumerate(copies):

        @pl.when(valid)
        def _(i=i):
            load(i).wait()
            store(i).start()

    for i, (valid, _, _) in enumerate(copies):

        @pl.when(valid)
        def _(i=i):
            store(i).wait()


def at_least_zero(index):
    return jnp.maximum(index, 0)


def staging(count, shape, dtype):
    return [
        pltpu.VMEM((count,) + shape, dtype),
        pltpu.SemaphoreType.DMA((count,)),
        pltpu.SemaphoreType.DMA((count,)),
    ]


def choose(index, refs, start, rows):
    found, first = [], 0
    for ref in refs:
        count = ref.shape[0]
        here = (index >= first) & (index < first + count)
        piece = jnp.clip(index - first, 0, count - 1)
        found.append((here, ref.at[piece, pl.ds(start, rows)]))
        first += count
    return found


def spread_kernel(parts, sizes, start, index_ref, *refs):
    sources, outs = refs[:parts], refs[parts : parts + len(sizes)]
    targets = [out.at[i] for out in outs for i in range(out.shape[0])]
    copies = []
    for i, target in enumerate(targets):
        for valid, piece in choose(index_ref[i], sources, start, outs[0].shape[1]):
            copies.append((valid, piece, target))
    stage(copies, *refs[parts + len(sizes) :])


def spread(sources, index, sizes, start, rows):
    count, piece = sum(sizes), (rows, sources[0].shape[2])
    dtype = sources[0].dtype
    any_space = pl.BlockSpec(memory_space=pl.ANY)
    return pl.pallas_call(
        functools.partial(spread_kernel, len(sources), sizes, start),
        out_shape=[jax.ShapeDtypeStruct((n,) + piece, dtype) for n in sizes],
        in_specs=[pl.BlockSpec(memory_space=pltpu.SMEM)] + [any_space] * len(sources),
        out_specs=[any_space] * len(sizes),
        scratch_shapes=staging(count * len(sources), piece, dtype),
        compiler_params=pltpu.CompilerParams(vmem_limit_bytes=VMEM_LIMIT),
        cost_estimate=pl.CostEstimate(
            flops=0, bytes_accessed=4 * count * piece[0] * piece[1], transcendentals=0
        ),
        name="spread",
    )(index, *sources)


def collect_kernel(parts, start, to_ref, *refs):
    sources, out = refs[:parts], refs[parts]
    rows = out.shape[1]
    pieces = []
    for ref in sources:
        first = start if ref.shape[1] > rows else 0
        pieces += [ref.at[i, pl.ds(first, rows)] for i in range(ref.shape[0])]
    copies = []
    for i, piece in enumerate(pieces):
        to = to_ref[i]
        copies.append((to >= 0, piece, out.at[at_least_zero(to)]))
    stage(copies, *refs[parts + 1 :])


def collect(sources, start, rows, to, count):
    piece = (rows, sources[0].shape[2])
    dtype = sources[0].dtype
    any_space = pl.BlockSpec(memory_space=pl.ANY)
    return pl.pallas_call(
        functools.partial(collect_kernel, len(sources), start),
        out_shape=jax.ShapeDtypeStruct((count,) + piece, dtype),
        in_specs=[pl.BlockSpec(memory_space=pltpu.SMEM)] + [any_space] * len(sources),
        out_specs=any_space,
        scratch_shapes=staging(to.shape[0], piece, dtype),
        compiler_params=pltpu.CompilerParams(vmem_limit_bytes=VMEM_LIMIT),
        cost_estimate=pl.CostEstimate(
            flops=0, bytes_accessed=4 * count * piece[0] * piece[1], transcendentals=0
        ),
        name="collect",
    )(to, *sources)


def precondition_kernel(chunks, left_ref, right_ref, *refs):
    grads, outs = refs[:chunks], refs[chunks : 2 * chunks]
    block, product = refs[2 * chunks :]
    size = block.shape[0]
    for c in range(chunks):
        piece = grads[c].shape[2]
        for d in range(grads[c].shape[0]):
            start = (d * chunks + c) * piece
            block[start : start + piece, :] = grads[c][d, 0]
    grad_sum = jnp.zeros((1, size), jnp.float32)
    prod_sum = jnp.zeros((1, size), jnp.float32)
    for i in range(size // STRIP):
        rows = slice(i * STRIP, (i + 1) * STRIP)
        left_part = jnp.dot(
            left_ref[0, rows, :], block[...], preferred_element_type=jnp.float32
        ).astype(jnp.bfloat16)
        strip = jnp.dot(left_part, right_ref[0], preferred_element_type=jnp.float32)
        product[rows, :] = strip
        prod_sum += jnp.sum(strip * strip, axis=0, keepdims=True)
        grad = block[rows, :].astype(jnp.float32)
        grad_sum += jnp.sum(grad * grad, axis=0, keepdims=True)
    scale = 1.0 / (size * size)
    grad_norm = jnp.sqrt(jnp.sum(grad_sum, axis=1, keepdims=True) * scale)
    prod_norm = jnp.sqrt(jnp.sum(prod_sum, axis=1, keepdims=True) * scale + 1e-06)
    ratio = grad_norm / prod_norm
    for c in range(chunks):
        piece = outs[c].shape[2]
        for d in range(outs[c].shape[0]):
            start = (d * chunks + c) * piece
            outs[c][d, 0] = (product[start : start + piece, :] * ratio).astype(jnp.bfloat16)


def precondition(left_root, right_root, pieces):
    slots, size, _ = left_root.shape
    chunks = len(pieces)
    root_spec = pl.BlockSpec((1, size, size), lambda s: (s, 0, 0))
    part = pieces[0].shape
    part_spec = pl.BlockSpec((part[0], 1) + part[2:], lambda s: (0, s, 0, 0))
    return pl.pallas_call(
        functools.partial(precondition_kernel, chunks),
        grid=(slots,),
        out_shape=[jax.ShapeDtypeStruct(part, jnp.bfloat16)] * chunks,
        in_specs=[root_spec, root_spec] + [part_spec] * chunks,
        out_specs=[part_spec] * chunks,
        scratch_shapes=[
            pltpu.VMEM((size, size), jnp.bfloat16),
            pltpu.VMEM((size, size), jnp.float32),
        ],
        compiler_params=pltpu.CompilerParams(vmem_limit_bytes=VMEM_LIMIT),
        cost_estimate=pl.CostEstimate(
            flops=4 * slots * size**3, bytes_accessed=8 * slots * size * size, transcendentals=0
        ),
        name="precondition",
    )(left_root, right_root, *pieces)


def update_kernel(parts, from_ref, to_ref, momentum_ref, *refs):
    out, buffer, loads = refs[parts * CHUNKS :]
    rows = out.shape[1] // CHUNKS
    own = from_ref.shape[0]
    copies = []
    for c in range(CHUNKS):
        near, far = refs[c * parts : c * parts + 2], refs[c * parts + 2 : (c + 1) * parts]
        pieces = []
        for i in range(own):
            for valid, piece in choose(from_ref[i], near, 0, rows):
                pieces.append((valid, piece, i))
        for k, piece in enumerate([ref.at[i] for ref in far for i in range(ref.shape[0])]):
            pieces.append((True, piece, own + k))
        for n, (valid, piece, i) in enumerate(pieces):
            to = to_ref[i]
            target = buffer.at[at_least_zero(to), pl.ds(c * rows, rows)]
            copies.append((valid & (to >= 0), piece, target, loads.at[c, n]))

    for valid, piece, target, sem in copies:

        @pl.when(valid)
        def _(piece=piece, target=target, sem=sem):
            pltpu.make_async_copy(piece, target, sem).start()

    for valid, piece, target, sem in copies:

        @pl.when(valid)
        def _(piece=piece, target=target, sem=sem):
            pltpu.make_async_copy(piece, target, sem).wait()

    for j in range(buffer.shape[0]):
        out[j] = 0.9 * momentum_ref[j] + buffer[j].astype(jnp.float32)


def update(momentum, near_from, to, chunks):
    vmem_space = pl.BlockSpec(memory_space=pltpu.VMEM)
    arrays = [x for chunk in chunks for x in chunk]
    return pl.pallas_call(
        functools.partial(update_kernel, len(chunks[0])),
        out_shape=jax.ShapeDtypeStruct(momentum.shape, jnp.float32),
        in_specs=[pl.BlockSpec(memory_space=pltpu.SMEM)] * 2
        + [vmem_space]
        + [pl.BlockSpec(memory_space=pl.ANY)] * len(arrays),
        out_specs=vmem_space,
        scratch_shapes=[
            pltpu.VMEM(momentum.shape, arrays[0].dtype),
            pltpu.SemaphoreType.DMA((CHUNKS, to.shape[0] + near_from.shape[0])),
        ],
        compiler_params=pltpu.CompilerParams(vmem_limit_bytes=VMEM_LIMIT),
        name="update",
    )(near_from, to, momentum, *arrays)


def table(match, values):
    return jnp.sum(jnp.where(match, values + 1, 0), axis=-1).astype(jnp.int32) - 1


def exchange(pieces, count):
    shape = pieces.shape
    pieces = pieces.reshape(count, -1, shape[-1])
    pieces = lax.all_to_all(pieces, "dp", split_axis=0, concat_axis=0, tiled=True)
    return pieces.reshape(shape)


def swap(piece, distance):
    groups = lax.axis_size("group")
    return lax.ppermute(piece, "group", [(g, g ^ distance) for g in range(groups)])


def shards(grad_partial, left_root, right_root, block_owner, momentum):
    dp_count = lax.axis_size("dp")
    groups = lax.axis_size("group")
    group_index = lax.axis_index("group")
    slot_count = left_root.shape[0]
    local_count, row_count, col_count = momentum.shape
    block_total = block_owner.shape[0]
    rows = lax.psum_scatter(grad_partial, "dp", scatter_dimension=2, tiled=True)[0]

    block_ids = jnp.arange(block_total, dtype=jnp.int32)
    owner_device = block_owner // slot_count
    owner_group = owner_device % groups
    owner_place = owner_device // groups * slot_count + block_owner % slot_count
    source_group = block_ids // local_count
    owner_chip = owner_group // 2
    chips = groups // 2
    earlier = (
        (block_ids[None, :] < block_ids[:, None])
        & (source_group[None, :] == source_group[:, None])
        & (owner_chip[None, :] == owner_chip[:, None])
    )
    rank_in = jnp.sum(earlier.astype(jnp.int32), axis=1)
    places = dp_count * slot_count
    offsets = 2 * jnp.arange(chips, dtype=jnp.int32)[:, None, None]
    ranked = rank_in[None, None, :] == jnp.arange(CAP, dtype=jnp.int32)[None, :, None]
    owned = (owner_group == group_index)[None, None, :]
    source = source_group[None, None, :]
    mine = table(
        (source == group_index)
        & (owner_chip[None, None, :] == (group_index ^ offsets) // 2)
        & ranked,
        block_ids - group_index * local_count,
    )
    same_to = table((source == group_index ^ offsets) & owned & ranked, owner_place)
    other_to = table((source == group_index ^ offsets ^ 1) & owned & ranked, owner_place)
    numbers = jnp.arange(local_count, dtype=jnp.int32)[:, None]
    own_to, near_to = [
        table((block_ids[None, :] == g * local_count + numbers) & owned[0], owner_place)
        for g in (group_index, group_index ^ 1)
    ]
    to_place = jnp.concatenate(
        [own_to, near_to, same_to[1:].reshape(-1), other_to[1:].reshape(-1)]
    )
    back_from = table(
        (source == group_index ^ offsets)
        & (owner_chip[None, None, :] == group_index // 2)
        & ranked,
        owner_place + jnp.where(owner_group == group_index, 0, places),
    )

    piece = row_count // CHUNKS
    sizes = [CAP] * (chips - 1)
    near = swap(rows, 1)
    came = []
    after = None
    for c in range(CHUNKS):
        sent = spread([rows], mine[1:].reshape(-1), sizes, c * piece, piece)
        if after is not None:
            *sent, after = lax.optimization_barrier((*sent, after))
            came.append(exchange(after, dp_count))
        same = [swap(sent[q - 1], 2 * q) for q in range(1, chips)]
        other = [swap(x, 1) for x in same]
        after = collect([rows, near] + same + other, c * piece, piece, to_place, places)
    came.append(exchange(after, dp_count))
    came = [x.reshape(dp_count, slot_count, piece, col_count) for x in came]
    chunks = []
    for direction in precondition(left_root, right_root, came):
        back = exchange(direction.reshape(places, piece, col_count), dp_count)
        back = [back, swap(back, 1)]
        sent = spread(back, back_from[1:].reshape(-1), sizes, 0, piece)
        chunks.append(back + [swap(sent[q - 1], 2 * q) for q in range(1, chips)])
    return update(momentum, back_from[0], mine.reshape(-1), chunks)


def solution(mesh):
    return jax.shard_map(
        shards,
        mesh=mesh,
        in_specs=(
            P("dp", "group", None, None),
            P(("dp", "group"), None, None),
            P(("dp", "group"), None, None),
            P(),
            P("group", "dp", None),
        ),
        out_specs=P("group", "dp", None),
        check_vma=False,
    )
```

time: 438 us -> 339 us (0.77)
  waiting for transfers between devices: 228 us -> 174 us
  Pallas kernels: 71.8 us -> 25.9 us
  blocking collectives: 89.9 us -> 110 us
  starting transfers between devices: 21.7 us -> 9.56 us
  local copies, waits for them, and re-layouts: 11 us -> 4.28 us
    unnamed x4 -> x1, waiting for transfers between devices: 151 us -> 0.71 us
    reduce_scatter x0 -> x1, waiting for transfers between devices: none -> 107 us  [shards(): lax.psum_scatter(grad_partial, 'dp', scatter_dimension=2, tiled=True)[0]]
    all_to_all x5 -> x0, waiting for transfers between devices: 76.9 us -> none  [the longest x2 39.8 us: shards(): came = lax.all_to_all(sent, 'dp', split_axis=0, concat_axis=0, tiled=True)]
    ppermute x0 -> x11, waiting for transfers between devices: none -> 66.1 us  [swap(): lax.ppermute(piece, 'group', [(g, g ^ distance) for g in range(groups)])]
    pallas_call x9 -> x4, Pallas kernels: 59 us -> 12.9 us  [the longest x2 5.55 us: spread(): pl.pallas_call(functools.partial(spread_kernel, len(sources), sizes, star...]
    all_to_all x5 -> x0, starting transfers between devices: 21.6 us -> none  [the longest x3 12.9 us: shards(): lax.all_to_all(sent, 'group', split_axis=0, concat_axis=0, tiled=True)]
    all_to_all x3 -> x2, blocking collectives: 89.9 us -> 110 us  [exchange(): lax.all_to_all(pieces, 'dp', split_axis=0, concat_axis=0, tiled=True)]
    ppermute x0 -> x11, starting transfers between devices: none -> 9.56 us  [swap(): lax.ppermute(piece, 'group', [(g, g ^ distance) for g in range(groups)])]
  transfers between devices with their start and end apart: 7 -> 12, of which waited for: 6 -> 9; matrix products, arithmetic and copies ran while one was open for 0% -> 1% of each run, Pallas kernels for 11% -> 0%
where the time goes in v3:
time: 339 us
  waiting for transfers between devices  174 us (51%)
  blocking collectives  110 us (32%)
  Pallas kernels  25.9 us (8%)
  between operations  13.6 us (4%)
  starting transfers between devices  9.56 us (3%)
  local copies, waits for them, and re-layouts  4.28 us (1%)
    all_to_all x2, blocking collectives, exchange(): lax.all_to_all(pieces, 'dp', split_axis=0, concat_axis=0, tiled=True)  110 us
    reduce_scatter x1, waiting for transfers between devices, shards(): lax.psum_scatter(grad_partial, 'dp', scatter_dimension=2, tiled=True)[0]  107 us
    ppermute x11, waiting for transfers between devices, swap(): lax.ppermute(piece, 'group', [(g, g ^ distance) for g in range(groups)])  66.1 us
    pallas_call x1, Pallas kernels, precondition(): pl.pallas_call(functools.partial(precondition_kernel, chunks), grid=(slot...  13 us
    ppermute x11, starting transfers between devices, swap(): lax.ppermute(piece, 'group', [(g, g ^ distance) for g in range(groups)])  9.56 us
  transfers between devices with their start and end apart: 12, of which 9 were waited for; matrix products, arithmetic and copies ran while one was open for 1% of the time, Pallas kernels for 0%

profile of v3, /device:TPU:0, one launch (start us, length us, event | category | flops | bytes accessed | tf_op | source)
XLA Modules:
  0.0 339.0 jit_solution(10987879717235271360)
XLA Ops:
  6.5 0.7 reduce-scatter.2.cloned.1.call-update
  7.4 0.2 convert_reduce_fusion
  7.8 0.4 select_reduce_fusion.1
  8.5 106.7 %reduce-scatter.2.cloned.1.call-done = bf16[1,7,64,1024]{3,2,1,0:T(8,128)(2,1)} async-done(((bf16[1,7,1024,1024]{3,2,1,0:T(8,128)(2,1)}), bf16[1,7,64,1024]{3,2,1,0:T(8,128)(2,1)}) %reduce-scatter.2.cloned.1.call-update) | async-done | bytes 917520 | tf_op jit(solution)/shard_map/reduce_scatter | solution.py:258
  115.2 1.2 copy-done
  116.3 2.8 spread.2
  119.1 1.7 collective-permute-start.1
  120.8 2.6 collective-permute-start.2
  123.4 0.5 collective-permute-start.3
  124.0 0.1 copy.12
  124.1 0.7 reshape.316
  125.0 12.0 %collective-permute-done.1.refs_2_ = bf16[5,64,1024]{2,1,0:T(8,128)(2,1)S(1)} collective-permute-done((bf16[5,64,1024]{2,1,0:T(8,128)(2,1)}, bf16[5,64,1024]{2,1,0:T(8,128)(2,1)S(1)}, u32[]{:S(2)}, u32[]{:S(2)}) %collective-permute-start.1) | collective-permute-done | bytes 655392 | tf_op jit(solution)/shard_map/ppermute | solution.py:248
  137.0 14.9 %collective-permute-done.2.refs_3_ = bf16[5,64,1024]{2,1,0:T(8,128)(2,1)S(1)} collective-permute-done((bf16[5,64,1024]{2,1,0:T(8,128)(2,1)}, bf16[5,64,1024]{2,1,0:T(8,128)(2,1)S(1)}, u32[]{:S(2)}, u32[]{:S(2)}) %collective-permute-start.2) | collective-permute-done | bytes 655392 | tf_op jit(solution)/shard_map/ppermute | solution.py:248
  151.9 2.4 collective-permute-done.3.refs_4_
  154.2 0.9 select_reduce_fusion.5
  155.1 0.8 pad_add_fusion.to_ref
  155.9 0.4 collective-permute-done.6.refs_7_
  156.3 1.2 copy-done.1
  157.5 3.1 collect.1
  160.6 56.2 %all_to_all.10 = bf16[16,128,1024]{2,1,0:T(8,128)(2,1)} all-to-all(bf16[16,128,1024]{2,1,0:T(8,128)(2,1)} %bitcast.9), channel_id=1, replica_groups=mesh['dp'=16,'group'=8] {'dp'}, dimensions={0} | all-to-all | bytes 8388608 | tf_op jit(solution)/shard_map/all_to_all | solution.py:242
  216.8 13.0 %precondition.1 = bf16[16,2,64,1024]{3,2,1,0:T(8,128)(2,1)S(1)} custom-call(bf16[2,1024,1024]{2,1,0:T(8,128)(2,1)} %left_ref.1, bf16[2,1024,1024]{2,1,0:T(8,128)(2,1)} %right_ref.1, bf16[16,2,64,1024]{3,2,1,0:T(8,128)(2,1)} %bitcast.10), custom_call_target="tpu_custom_call" | custom-call | flops 8589934592 | bytes 16777216 | tf_op jit(solution)/shard_map/precondition/pallas_call | solution.py:164
  229.8 53.4 %all_to_all.11 = bf16[16,128,1024]{2,1,0:T(8,128)(2,1)} all-to-all(bf16[16,128,1024]{2,1,0:T(8,128)(2,1)S(1)} %bitcast.5), channel_id=1, replica_groups=mesh['dp'=16,'group'=8] {'dp'}, dimensions={0} | all-to-all | bytes 8388608 | tf_op jit(solution)/shard_map/all_to_all | solution.py:242
  283.3 0.1 copy.15
  283.5 7.2 %collective-permute-done.7.refs_1_ = bf16[32,64,1024]{2,1,0:T(8,128)(2,1)} collective-permute-done((bf16[32,64,1024]{2,1,0:T(8,128)(2,1)}, bf16[32,64,1024]{2,1,0:T(8,128)(2,1)}, u32[]{:S(2)}, u32[]{:S(2)}) %collective-permute-start.7) | collective-permute-done | bytes 4194336 | tf_op jit(solution)/shard_map/ppermute | solution.py:248
  290.7 2.8 spread.3
  293.6 2.4 collective-permute-start.9
  296.0 2.3 collective-permute-start.10
  298.5 0.1 slice_reduce_fusion.from_ref
  298.6 12.8 %collective-permute-done.8.refs_2_ = bf16[5,64,1024]{2,1,0:T(8,128)(2,1)S(1)} collective-permute-done((bf16[5,64,1024]{2,1,0:T(8,128)(2,1)}, bf16[5,64,1024]{2,1,0:T(8,128)(2,1)S(1)}, u32[]{:S(2)}, u32[]{:S(2)}) %collective-permute-start.8) | collective-permute-done | bytes 655392 | tf_op jit(solution)/shard_map/ppermute | solution.py:248
  311.4 13.8 %collective-permute-done.9.refs_3_ = bf16[5,64,1024]{2,1,0:T(8,128)(2,1)S(1)} collective-permute-done((bf16[5,64,1024]{2,1,0:T(8,128)(2,1)}, bf16[5,64,1024]{2,1,0:T(8,128)(2,1)S(1)}, u32[]{:S(2)}, u32[]{:S(2)}) %collective-permute-start.9) | collective-permute-done | bytes 655392 | tf_op jit(solution)/shard_map/ppermute | solution.py:248
  325.2 2.7 collective-permute-done.10.refs_4_
  327.9 4.3 %update.1 = f32[7,64,1024]{2,1,0:T(8,128)} custom-call(s32[5]{0:T(128)S(1)} %slice_reduce_fusion.from_ref, s32[20]{0:T(128)S(1)} %sub.68.to_ref, f32[7,64,1024]{2,1,0:T(8,128)S(1)} %copy-done.2, bf16[32,64,1024]{2,1,0:T(8,128)(2,1)} %bitcast.4.refs_0_, bf16[32,64,1024]{2,1,0:T(8,128)(2,1)} %collective-permute-done.7.refs_1_, ...), custom_call_target="tpu_custom_call" | custom-call | tf_op jit(solution)/shard_map/update/pallas_call | solution.py:219
  (48 shorter events, 1.3 us)
Async XLA Ops:
  6.5 0.8 copy-start.4
  6.5 108.6 %reduce-scatter.2.cloned.1.call-start = ((), (), s32[]{:S(2)}) async-start(), calls=%async_computation.3 | async-start | bytes 15597568 | tf_op jit(solution)/shard_map/reduce_scatter | solution.py:258
  7.4 0.8 copy-start.3
  7.6 0.6 copy-start.5
  115.2 1.2 copy-start
  119.1 17.9 %collective-permute-start.1 = (bf16[5,64,1024]{2,1,0:T(8,128)(2,1)}, bf16[5,64,1024]{2,1,0:T(8,128)(2,1)S(1)}, u32[]{:S(2)}, u32[]{:S(2)}) collective-permute-start(bf16[5,64,1024]{2,1,0:T(8,128)(2,1)} %get-tuple-element.11), channel_id=1, source_target_pairs={{0,2},{1,3},{2,0},{3,1},{4,6},{5,7},{6,4},{7,5},{8,10},{9,11},{10,... | collective-permute-start | bytes 1966088 | tf_op jit(solution)/shard_map/ppermute | solution.py:248
  120.8 31.1 %collective-permute-start.2 = (bf16[5,64,1024]{2,1,0:T(8,128)(2,1)}, bf16[5,64,1024]{2,1,0:T(8,128)(2,1)S(1)}, u32[]{:S(2)}, u32[]{:S(2)}) collective-permute-start(bf16[5,64,1024]{2,1,0:T(8,128)(2,1)} %get-tuple-element.12), channel_id=1, source_target_pairs={{0,4},{1,5},{2,6},{3,7},{4,0},{5,1},{6,2},{7,3},{8,12},{9,13},{10,... | collective-permute-start | bytes 1966088 | tf_op jit(solution)/shard_map/ppermute | solution.py:248
  123.4 30.9 %collective-permute-start.3 = (bf16[5,64,1024]{2,1,0:T(8,128)(2,1)S(1)}, bf16[5,64,1024]{2,1,0:T(8,128)(2,1)S(1)}, u32[]{:S(2)}, u32[]{:S(2)}) collective-permute-start(bf16[5,64,1024]{2,1,0:T(8,128)(2,1)S(1)} %get-tuple-element.13), channel_id=1, source_target_pairs={{0,6},{1,7},{2,4},{3,5},{4,2},{5,3},{6,0},{7,1},{8,14},{9,15},{10,... | collective-permute-start | bytes 1966088 | tf_op jit(solution)/shard_map/ppermute | solution.py:248
  124.7 31.2 %collective-permute-start = (bf16[7,64,1024]{2,1,0:T(8,128)(2,1)}, bf16[7,64,1024]{2,1,0:T(8,128)(2,1)S(1)}, u32[]{:S(2)}, u32[]{:S(2)}) collective-permute-start(bf16[7,64,1024]{2,1,0:T(8,128)(2,1)} %bitcast.6), channel_id=1, source_target_pairs={{0,1},{1,0},{2,3},{3,2},{4,5},{5,4},{6,7},{7,6},{8,9},{9,8},{10,11... | collective-permute-start | bytes 2752520 | tf_op jit(solution)/shard_map/ppermute | solution.py:248
  137.0 18.9 %collective-permute-start.4 = (bf16[5,64,1024]{2,1,0:T(8,128)(2,1)S(1)}, bf16[5,64,1024]{2,1,0:T(8,128)(2,1)S(1)}, u32[]{:S(2)}, u32[]{:S(2)}) collective-permute-start(bf16[5,64,1024]{2,1,0:T(8,128)(2,1)S(1)} %collective-permute-done.1.refs_2_), channel_id=1, source_target_pairs={{0,1},{1,0},{2,3},{3,2},{4,5},{5,4},{6,7},{7,6},{8,9},{9,8},{10,11... | collective-permute-start | bytes 1966088 | tf_op jit(solution)/shard_map/ppermute | solution.py:248
  151.9 4.0 %collective-permute-start.5 = (bf16[5,64,1024]{2,1,0:T(8,128)(2,1)S(1)}, bf16[5,64,1024]{2,1,0:T(8,128)(2,1)S(1)}, u32[]{:S(2)}, u32[]{:S(2)}) collective-permute-start(bf16[5,64,1024]{2,1,0:T(8,128)(2,1)S(1)} %collective-permute-done.2.refs_3_), channel_id=1, source_target_pairs={{0,1},{1,0},{2,3},{3,2},{4,5},{5,4},{6,7},{7,6},{8,9},{9,8},{10,11... | collective-permute-start | bytes 1966088 | tf_op jit(solution)/shard_map/ppermute | solution.py:248
  154.2 2.1 collective-permute-start.6
  156.3 1.2 copy-start.1
  283.2 7.5 %collective-permute-start.7 = (bf16[32,64,1024]{2,1,0:T(8,128)(2,1)}, bf16[32,64,1024]{2,1,0:T(8,128)(2,1)}, u32[]{:S(2)}, u32[]{:S(2)}) collective-permute-start(bf16[32,64,1024]{2,1,0:T(8,128)(2,1)} %bitcast.4.refs_0_), channel_id=1, source_target_pairs={{0,1},{1,0},{2,3},{3,2},{4,5},{5,4},{6,7},{7,6},{8,9},{9,8},{10,11... | collective-permute-start | bytes 12582920 | tf_op jit(solution)/shard_map/ppermute | solution.py:248
  283.5 44.4 %copy-start.2 = (f32[7,64,1024]{2,1,0:T(8,128)S(1)}, f32[7,64,1024]{2,1,0:T(8,128)}, u32[]{:S(2)}) copy-start(f32[7,64,1024]{2,1,0:T(8,128)} %momentum_ref.1) | copy-start | bytes 5505028
  293.5 17.9 %collective-permute-start.8 = (bf16[5,64,1024]{2,1,0:T(8,128)(2,1)}, bf16[5,64,1024]{2,1,0:T(8,128)(2,1)S(1)}, u32[]{:S(2)}, u32[]{:S(2)}) collective-permute-start(bf16[5,64,1024]{2,1,0:T(8,128)(2,1)} %get-tuple-element.14), channel_id=1, source_target_pairs={{0,2},{1,3},{2,0},{3,1},{4,6},{5,7},{6,4},{7,5},{8,10},{9,11},{10,... | collective-permute-start | bytes 1966088 | tf_op jit(solution)/shard_map/ppermute | solution.py:248
  293.6 31.6 %collective-permute-start.9 = (bf16[5,64,1024]{2,1,0:T(8,128)(2,1)}, bf16[5,64,1024]{2,1,0:T(8,128)(2,1)S(1)}, u32[]{:S(2)}, u32[]{:S(2)}) collective-permute-start(bf16[5,64,1024]{2,1,0:T(8,128)(2,1)} %get-tuple-element.15), channel_id=1, source_target_pairs={{0,4},{1,5},{2,6},{3,7},{4,0},{5,1},{6,2},{7,3},{8,12},{9,13},{10,... | collective-permute-start | bytes 1966088 | tf_op jit(solution)/shard_map/ppermute | solution.py:248
  296.0 31.8 %collective-permute-start.10 = (bf16[5,64,1024]{2,1,0:T(8,128)(2,1)}, bf16[5,64,1024]{2,1,0:T(8,128)(2,1)}, u32[]{:S(2)}, u32[]{:S(2)}) collective-permute-start(bf16[5,64,1024]{2,1,0:T(8,128)(2,1)} %get-tuple-element.16), channel_id=1, source_target_pairs={{0,6},{1,7},{2,4},{3,5},{4,2},{5,3},{6,0},{7,1},{8,14},{9,15},{10,... | collective-permute-start | bytes 1966088 | tf_op jit(solution)/shard_map/ppermute | solution.py:248
Sparse Core Ops, SparseCore 0:
  10.8 104.3 reduce-scatter.1

commit v4 on v3

--- a/solution.py
+++ b/solution.py
@@ -11,6 +11,7 @@
 CHUNKS = 1
 STRIP = 256
 VMEM_LIMIT = 48 * 1024 * 1024
+PRODUCT_VMEM_LIMIT = 32 * 1024 * 1024
 
 
 def stage(copies, buffer, loads, stores):
@@ -123,60 +124,55 @@
     )(to, *sources)
 
 
-def precondition_kernel(chunks, left_ref, right_ref, *refs):
-    grads, outs = refs[:chunks], refs[chunks : 2 * chunks]
-    block, product = refs[2 * chunks :]
+def precondition_kernel(left_ref, right_ref, grad_ref, out_ref, block, product):
     size = block.shape[0]
-    for c in range(chunks):
-        piece = grads[c].shape[2]
-        for d in range(grads[c].shape[0]):
-            start = (d * chunks + c) * piece
-            block[start : start + piece, :] = grads[c][d, 0]
-    grad_sum = jnp.zeros((1, size), jnp.float32)
-    prod_sum = jnp.zeros((1, size), jnp.float32)
-    for i in range(size // STRIP):
-        rows = slice(i * STRIP, (i + 1) * STRIP)
-        left_part = jnp.dot(
-            left_ref[0, rows, :], block[...], preferred_element_type=jnp.float32
-        ).astype(jnp.bfloat16)
-        strip = jnp.dot(left_part, right_ref[0], preferred_element_type=jnp.float32)
-        product[rows, :] = strip
-        prod_sum += jnp.sum(strip * strip, axis=0, keepdims=True)
-        grad = block[rows, :].astype(jnp.float32)
-        grad_sum += jnp.sum(grad * grad, axis=0, keepdims=True)
-    scale = 1.0 / (size * size)
-    grad_norm = jnp.sqrt(jnp.sum(grad_sum, axis=1, keepdims=True) * scale)
-    prod_norm = jnp.sqrt(jnp.sum(prod_sum, axis=1, keepdims=True) * scale + 1e-06)
-    ratio = grad_norm / prod_norm
-    for c in range(chunks):
-        piece = outs[c].shape[2]
-        for d in range(outs[c].shape[0]):
-            start = (d * chunks + c) * piece
-            outs[c][d, 0] = (product[start : start + piece, :] * ratio).astype(jnp.bfloat16)
+    places, _, piece, _ = grad_ref.shape
+
+    def one_slot(s, carry):
+        for d in range(places):
+            block[d * piece : (d + 1) * piece, :] = grad_ref[d, s]
+        grad_sum = jnp.zeros((1, size), jnp.float32)
+        prod_sum = jnp.zeros((1, size), jnp.float32)
+        for i in range(size // STRIP):
+            rows = slice(i * STRIP, (i + 1) * STRIP)
+            left_part = jnp.dot(
+                left_ref[s, rows, :], block[...], preferred_element_type=jnp.float32
+            ).astype(jnp.bfloat16)
+            strip = jnp.dot(left_part, right_ref[s], preferred_element_type=jnp.float32)
+            product[rows, :] = strip
+            prod_sum += jnp.sum(strip * strip, axis=0, keepdims=True)
+            grad = block[rows, :].astype(jnp.float32)
+            grad_sum += jnp.sum(grad * grad, axis=0, keepdims=True)
+        scale = 1.0 / (size * size)
+        grad_norm = jnp.sqrt(jnp.sum(grad_sum, axis=1, keepdims=True) * scale)
+        prod_norm = jnp.sqrt(jnp.sum(prod_sum, axis=1, keepdims=True) * scale + 1e-06)
+        ratio = grad_norm / prod_norm
+        for d in range(places):
+            rows = slice(d * piece, (d + 1) * piece)
+            out_ref[d, s] = (product[rows, :] * ratio).astype(jnp.bfloat16)
+        return carry
+
+    lax.fori_loop(0, left_ref.shape[0], one_slot, 0)
 
 
 def precondition(left_root, right_root, pieces):
     slots, size, _ = left_root.shape
-    chunks = len(pieces)
-    root_spec = pl.BlockSpec((1, size, size), lambda s: (s, 0, 0))
-    part = pieces[0].shape
-    part_spec = pl.BlockSpec((part[0], 1) + part[2:], lambda s: (0, s, 0, 0))
+    vmem_space = pl.BlockSpec(memory_space=pltpu.VMEM)
     return pl.pallas_call(
-        functools.partial(precondition_kernel, chunks),
-        grid=(slots,),
-        out_shape=[jax.ShapeDtypeStruct(part, jnp.bfloat16)] * chunks,
-        in_specs=[root_spec, root_spec] + [part_spec] * chunks,
-        out_specs=[part_spec] * chunks,
+        precondition_kernel,
+        out_shape=jax.ShapeDtypeStruct(pieces.shape, jnp.bfloat16),
+        in_specs=[vmem_space] * 3,
+        out_specs=vmem_space,
         scratch_shapes=[
             pltpu.VMEM((size, size), jnp.bfloat16),
             pltpu.VMEM((size, size), jnp.float32),
         ],
-        compiler_params=pltpu.CompilerParams(vmem_limit_bytes=VMEM_LIMIT),
+        compiler_params=pltpu.CompilerParams(vmem_limit_bytes=PRODUCT_VMEM_LIMIT),
         cost_estimate=pl.CostEstimate(
             flops=4 * slots * size**3, bytes_accessed=8 * slots * size * size, transcendentals=0
         ),
         name="precondition",
-    )(left_root, right_root, *pieces)
+    )(left_root, right_root, pieces)
 
 
 def update_kernel(parts, from_ref, to_ref, momentum_ref, *refs):
@@ -314,7 +310,7 @@
     came.append(exchange(after, dp_count))
     came = [x.reshape(dp_count, slot_count, piece, col_count) for x in came]
     chunks = []
-    for direction in precondition(left_root, right_root, came):
+    for direction in [precondition(left_root, right_root, came[0])]:
         back = exchange(direction.reshape(places, piece, col_count), dp_count)
         back = [back, swap(back, 1)]
         sent = spread(back, back_from[1:].reshape(-1), sizes, 0, piece)

time: 339 us -> 336 us (level)
  blocking collectives: 110 us -> 98.8 us
    all_to_all x2, blocking collectives: 110 us -> 98.8 us  [exchange(): lax.all_to_all(pieces, 'dp', split_axis=0, concat_axis=0, tiled=True)]
    pallas_call x1, Pallas kernels: 3.1 us -> 9.79 us  [collect(): pl.pallas_call(functools.partial(collect_kernel, len(sources), start), ou...]
where the time goes in v4:
time: 336 us; the launch traced here: 334 us
  waiting for transfers between devices  175 us (52%)
  blocking collectives  98.8 us (29%)
  Pallas kernels  28.3 us (8%)
  between operations  13.6 us (4%)
  starting transfers between devices  11.5 us (3%)
  local copies, waits for them, and re-layouts  4.27 us (1%)
    reduce_scatter x1, waiting for transfers between devices, shards(): lax.psum_scatter(grad_partial, 'dp', scatter_dimension=2, tiled=True)[0]  107 us
    all_to_all x2, blocking collectives, exchange(): lax.all_to_all(pieces, 'dp', split_axis=0, concat_axis=0, tiled=True)  98.8 us
    ppermute x11, waiting for transfers between devices, swap(): lax.ppermute(piece, 'group', [(g, g ^ distance) for g in range(groups)])  68 us
    ppermute x11, starting transfers between devices, swap(): lax.ppermute(piece, 'group', [(g, g ^ distance) for g in range(groups)])  11.5 us
    pallas_call x1, Pallas kernels, precondition(): pl.pallas_call(precondition_kernel, out_shape=jax.ShapeDtypeStruct(pieces...  9.85 us
    pallas_call x1, Pallas kernels, collect(): pl.pallas_call(functools.partial(collect_kernel, len(sources), start), ou...  9.79 us
  transfers between devices with their start and end apart: 12, of which 9 were waited for; matrix products, arithmetic and copies ran while one was open for 1% of the time, Pallas kernels for 0%

profile of v4, /device:TPU:0, one launch (start us, length us, event | category | flops | bytes accessed | tf_op | source)
XLA Modules:
  0.0 334.4 jit_solution(17563678058749964246)
XLA Ops:
  6.5 0.7 reduce-scatter.2.cloned.1.call-update
  7.4 0.2 convert_reduce_fusion
  7.8 0.4 select_reduce_fusion.1
  8.3 0.1 copy.14
  8.5 106.7 %reduce-scatter.2.cloned.1.call-done = bf16[1,7,64,1024]{3,2,1,0:T(8,128)(2,1)} async-done(((bf16[1,7,1024,1024]{3,2,1,0:T(8,128)(2,1)}), bf16[1,7,64,1024]{3,2,1,0:T(8,128)(2,1)}) %reduce-scatter.2.cloned.1.call-update) | async-done | bytes 917520 | tf_op jit(solution)/shard_map/reduce_scatter | solution.py:254
  115.2 1.2 copy-done
  116.3 2.0 spread.2
  118.3 2.4 collective-permute-start.1
  120.7 2.7 collective-permute-start.2
  123.7 0.7 reshape.316
  124.4 0.1 copy.13
  124.6 11.9 %collective-permute-done.1.refs_2_ = bf16[5,64,1024]{2,1,0:T(8,128)(2,1)S(1)} collective-permute-done((bf16[5,64,1024]{2,1,0:T(8,128)(2,1)}, bf16[5,64,1024]{2,1,0:T(8,128)(2,1)S(1)}, u32[]{:S(2)}, u32[]{:S(2)}) %collective-permute-start.1) | collective-permute-done | bytes 655392 | tf_op jit(solution)/shard_map/ppermute | solution.py:244
  136.5 15.5 %collective-permute-done.2.refs_3_ = bf16[5,64,1024]{2,1,0:T(8,128)(2,1)S(1)} collective-permute-done((bf16[5,64,1024]{2,1,0:T(8,128)(2,1)}, bf16[5,64,1024]{2,1,0:T(8,128)(2,1)S(1)}, u32[]{:S(2)}, u32[]{:S(2)}) %collective-permute-start.2) | collective-permute-done | bytes 655392 | tf_op jit(solution)/shard_map/ppermute | solution.py:244
  152.1 2.4 collective-permute-done.3.refs_4_
  154.4 0.9 select_reduce_fusion.5
  155.4 0.7 pad_add_fusion.to_ref
  156.1 0.4 collective-permute-done.6.refs_7_
  156.5 1.2 copy-done.1
  157.7 9.8 %collect.1 = bf16[32,64,1024]{2,1,0:T(8,128)(2,1)} custom-call(s32[44]{0:T(128)S(1)} %pad_add_fusion.to_ref, bf16[7,64,1024]{2,1,0:T(8,128)(2,1)S(1)} %bitcast.9, bf16[7,64,1024]{2,1,0:T(8,128)(2,1)S(1)} %collective-permute-done.refs_1_, bf16[5,64,1024]{2,1,0:T(8,128)(2,1)S(1)} %collective-permute-done.1.refs_2_, ...), custom_call_target="tpu_custom_call" | custom-call | bytes 8388608 | tf_op jit(solution)/shard_map/collect/pallas_call | solution.py:113
  167.5 49.8 %all_to_all.10 = bf16[16,128,1024]{2,1,0:T(8,128)(2,1)S(1)} all-to-all(bf16[16,128,1024]{2,1,0:T(8,128)(2,1)} %bitcast.10), channel_id=1, replica_groups=mesh['dp'=16,'group'=8] {'dp'}, dimensions={0} | all-to-all | bytes 8388608 | tf_op jit(solution)/shard_map/all_to_all | solution.py:238
  217.3 9.9 %precondition.1 = bf16[16,2,64,1024]{3,2,1,0:T(8,128)(2,1)S(1)} custom-call(bf16[2,1024,1024]{2,1,0:T(8,128)(2,1)S(1)} %copy-done.3, bf16[2,1024,1024]{2,1,0:T(8,128)(2,1)S(1)} %copy-done.4, bf16[16,2,64,1024]{3,2,1,0:T(8,128)(2,1)S(1)} %bitcast.5), custom_call_target="tpu_custom_call" | custom-call | flops 8589934592 | bytes 16777216 | tf_op jit(solution)/shard_map/precondition/pallas_call | solution.py:161
  227.2 49.0 %all_to_all.11 = bf16[16,128,1024]{2,1,0:T(8,128)(2,1)} all-to-all(bf16[16,128,1024]{2,1,0:T(8,128)(2,1)S(1)} %bitcast.6), channel_id=1, replica_groups=mesh['dp'=16,'group'=8] {'dp'}, dimensions={0} | all-to-all | bytes 8388608 | tf_op jit(solution)/shard_map/all_to_all | solution.py:238
  276.4 7.2 %collective-permute-done.7.refs_1_ = bf16[32,64,1024]{2,1,0:T(8,128)(2,1)} collective-permute-done((bf16[32,64,1024]{2,1,0:T(8,128)(2,1)}, bf16[32,64,1024]{2,1,0:T(8,128)(2,1)}, u32[]{:S(2)}, u32[]{:S(2)}) %collective-permute-start.7) | collective-permute-done | bytes 4194336 | tf_op jit(solution)/shard_map/ppermute | solution.py:244
  283.7 3.2 spread.3
  286.9 3.5 %collective-permute-start.8 = (bf16[5,64,1024]{2,1,0:T(8,128)(2,1)}, bf16[5,64,1024]{2,1,0:T(8,128)(2,1)S(1)}, u32[]{:S(2)}, u32[]{:S(2)}) collective-permute-start(bf16[5,64,1024]{2,1,0:T(8,128)(2,1)} %get-tuple-element.14), channel_id=1, source_target_pairs={{0,2},{1,3},{2,0},{3,1},{4,6},{5,7},{6,4},{7,5},{8,10},{9,11},{10,... | collective-permute-start | bytes 1966088 | tf_op jit(solution)/shard_map/ppermute | solution.py:244
  290.5 1.8 collective-permute-start.9
  292.3 1.0 collective-permute-start.10
  293.4 0.1 slice_reduce_fusion.from_ref
  293.5 12.7 %collective-permute-done.8.refs_2_ = bf16[5,64,1024]{2,1,0:T(8,128)(2,1)S(1)} collective-permute-done((bf16[5,64,1024]{2,1,0:T(8,128)(2,1)}, bf16[5,64,1024]{2,1,0:T(8,128)(2,1)S(1)}, u32[]{:S(2)}, u32[]{:S(2)}) %collective-permute-start.8) | collective-permute-done | bytes 655392 | tf_op jit(solution)/shard_map/ppermute | solution.py:244
  306.2 15.2 %collective-permute-done.9.refs_3_ = bf16[5,64,1024]{2,1,0:T(8,128)(2,1)S(1)} collective-permute-done((bf16[5,64,1024]{2,1,0:T(8,128)(2,1)}, bf16[5,64,1024]{2,1,0:T(8,128)(2,1)S(1)}, u32[]{:S(2)}, u32[]{:S(2)}) %collective-permute-start.9) | collective-permute-done | bytes 655392 | tf_op jit(solution)/shard_map/ppermute | solution.py:244
  321.4 2.7 collective-permute-done.10.refs_4_
  324.1 3.4 %update.1 = f32[7,64,1024]{2,1,0:T(8,128)} custom-call(s32[5]{0:T(128)S(1)} %slice_reduce_fusion.from_ref, s32[20]{0:T(128)S(1)} %sub.68.to_ref, f32[7,64,1024]{2,1,0:T(8,128)S(1)} %copy-done.2, bf16[32,64,1024]{2,1,0:T(8,128)(2,1)} %bitcast.4.refs_0_, bf16[32,64,1024]{2,1,0:T(8,128)(2,1)} %collective-permute-done.7.refs_1_, ...), custom_call_target="tpu_custom_call" | custom-call | tf_op jit(solution)/shard_map/update/pallas_call | solution.py:215
  (52 shorter events, 1.3 us)
Async XLA Ops:
  6.5 0.8 copy-start.6
  6.5 108.6 %reduce-scatter.2.cloned.1.call-start = ((), (), s32[]{:S(2)}) async-start(), calls=%async_computation.3 | async-start | bytes 15597568 | tf_op jit(solution)/shard_map/reduce_scatter | solution.py:254
  7.4 0.8 copy-start.5
  7.6 0.6 copy-start.7
  115.2 1.2 copy-start
  118.3 18.2 %collective-permute-start.1 = (bf16[5,64,1024]{2,1,0:T(8,128)(2,1)}, bf16[5,64,1024]{2,1,0:T(8,128)(2,1)S(1)}, u32[]{:S(2)}, u32[]{:S(2)}) collective-permute-start(bf16[5,64,1024]{2,1,0:T(8,128)(2,1)} %get-tuple-element.11), channel_id=1, source_target_pairs={{0,2},{1,3},{2,0},{3,1},{4,6},{5,7},{6,4},{7,5},{8,10},{9,11},{10,... | collective-permute-start | bytes 1966088 | tf_op jit(solution)/shard_map/ppermute | solution.py:244
  120.7 31.3 %collective-permute-start.2 = (bf16[5,64,1024]{2,1,0:T(8,128)(2,1)}, bf16[5,64,1024]{2,1,0:T(8,128)(2,1)S(1)}, u32[]{:S(2)}, u32[]{:S(2)}) collective-permute-start(bf16[5,64,1024]{2,1,0:T(8,128)(2,1)} %get-tuple-element.12), channel_id=1, source_target_pairs={{0,4},{1,5},{2,6},{3,7},{4,0},{5,1},{6,2},{7,3},{8,12},{9,13},{10,... | collective-permute-start | bytes 1966088 | tf_op jit(solution)/shard_map/ppermute | solution.py:244
  123.5 31.0 %collective-permute-start.3 = (bf16[5,64,1024]{2,1,0:T(8,128)(2,1)S(1)}, bf16[5,64,1024]{2,1,0:T(8,128)(2,1)S(1)}, u32[]{:S(2)}, u32[]{:S(2)}) collective-permute-start(bf16[5,64,1024]{2,1,0:T(8,128)(2,1)S(1)} %get-tuple-element.13), channel_id=1, source_target_pairs={{0,6},{1,7},{2,4},{3,5},{4,2},{5,3},{6,0},{7,1},{8,14},{9,15},{10,... | collective-permute-start | bytes 1966088 | tf_op jit(solution)/shard_map/ppermute | solution.py:244
  124.3 31.8 %collective-permute-start = (bf16[7,64,1024]{2,1,0:T(8,128)(2,1)}, bf16[7,64,1024]{2,1,0:T(8,128)(2,1)S(1)}, u32[]{:S(2)}, u32[]{:S(2)}) collective-permute-start(bf16[7,64,1024]{2,1,0:T(8,128)(2,1)} %bitcast.7), channel_id=1, source_target_pairs={{0,1},{1,0},{2,3},{3,2},{4,5},{5,4},{6,7},{7,6},{8,9},{9,8},{10,11... | collective-permute-start | bytes 2752520 | tf_op jit(solution)/shard_map/ppermute | solution.py:244
  136.5 19.6 %collective-permute-start.4 = (bf16[5,64,1024]{2,1,0:T(8,128)(2,1)S(1)}, bf16[5,64,1024]{2,1,0:T(8,128)(2,1)S(1)}, u32[]{:S(2)}, u32[]{:S(2)}) collective-permute-start(bf16[5,64,1024]{2,1,0:T(8,128)(2,1)S(1)} %collective-permute-done.1.refs_2_), channel_id=1, source_target_pairs={{0,1},{1,0},{2,3},{3,2},{4,5},{5,4},{6,7},{7,6},{8,9},{9,8},{10,11... | collective-permute-start | bytes 1966088 | tf_op jit(solution)/shard_map/ppermute | solution.py:244
  152.1 4.0 %collective-permute-start.5 = (bf16[5,64,1024]{2,1,0:T(8,128)(2,1)S(1)}, bf16[5,64,1024]{2,1,0:T(8,128)(2,1)S(1)}, u32[]{:S(2)}, u32[]{:S(2)}) collective-permute-start(bf16[5,64,1024]{2,1,0:T(8,128)(2,1)S(1)} %collective-permute-done.2.refs_3_), channel_id=1, source_target_pairs={{0,1},{1,0},{2,3},{3,2},{4,5},{5,4},{6,7},{7,6},{8,9},{9,8},{10,11... | collective-permute-start | bytes 1966088 | tf_op jit(solution)/shard_map/ppermute | solution.py:244
  154.4 2.1 collective-permute-start.6
  156.5 1.2 copy-start.1
  167.5 49.8 %copy-start.3 = (bf16[2,1024,1024]{2,1,0:T(8,128)(2,1)S(1)}, bf16[2,1024,1024]{2,1,0:T(8,128)(2,1)}, u32[]{:S(2)}) copy-start(bf16[2,1024,1024]{2,1,0:T(8,128)(2,1)} %left_ref.1) | copy-start | bytes 12582916
  167.5 49.8 %copy-start.4 = (bf16[2,1024,1024]{2,1,0:T(8,128)(2,1)S(1)}, bf16[2,1024,1024]{2,1,0:T(8,128)(2,1)}, u32[]{:S(2)}) copy-start(bf16[2,1024,1024]{2,1,0:T(8,128)(2,1)} %right_ref.1) | copy-start | bytes 12582916
  276.2 7.5 %collective-permute-start.7 = (bf16[32,64,1024]{2,1,0:T(8,128)(2,1)}, bf16[32,64,1024]{2,1,0:T(8,128)(2,1)}, u32[]{:S(2)}, u32[]{:S(2)}) collective-permute-start(bf16[32,64,1024]{2,1,0:T(8,128)(2,1)} %bitcast.4.refs_0_), channel_id=1, source_target_pairs={{0,1},{1,0},{2,3},{3,2},{4,5},{5,4},{6,7},{7,6},{8,9},{9,8},{10,11... | collective-permute-start | bytes 12582920 | tf_op jit(solution)/shard_map/ppermute | solution.py:244
  276.4 47.6 %copy-start.2 = (f32[7,64,1024]{2,1,0:T(8,128)S(1)}, f32[7,64,1024]{2,1,0:T(8,128)}, u32[]{:S(2)}) copy-start(f32[7,64,1024]{2,1,0:T(8,128)} %momentum_ref.1) | copy-start | bytes 5505028
  286.9 19.3 %collective-permute-start.8 = (bf16[5,64,1024]{2,1,0:T(8,128)(2,1)}, bf16[5,64,1024]{2,1,0:T(8,128)(2,1)S(1)}, u32[]{:S(2)}, u32[]{:S(2)}) collective-permute-start(bf16[5,64,1024]{2,1,0:T(8,128)(2,1)} %get-tuple-element.14), channel_id=1, source_target_pairs={{0,2},{1,3},{2,0},{3,1},{4,6},{5,7},{6,4},{7,5},{8,10},{9,11},{10,... | collective-permute-start | bytes 1966088 | tf_op jit(solution)/shard_map/ppermute | solution.py:244
  290.5 30.9 %collective-permute-start.9 = (bf16[5,64,1024]{2,1,0:T(8,128)(2,1)}, bf16[5,64,1024]{2,1,0:T(8,128)(2,1)S(1)}, u32[]{:S(2)}, u32[]{:S(2)}) collective-permute-start(bf16[5,64,1024]{2,1,0:T(8,128)(2,1)} %get-tuple-element.15), channel_id=1, source_target_pairs={{0,4},{1,5},{2,6},{3,7},{4,0},{5,1},{6,2},{7,3},{8,12},{9,13},{10,... | collective-permute-start | bytes 1966088 | tf_op jit(solution)/shard_map/ppermute | solution.py:244
  292.3 31.8 %collective-permute-start.10 = (bf16[5,64,1024]{2,1,0:T(8,128)(2,1)}, bf16[5,64,1024]{2,1,0:T(8,128)(2,1)}, u32[]{:S(2)}, u32[]{:S(2)}) collective-permute-start(bf16[5,64,1024]{2,1,0:T(8,128)(2,1)} %get-tuple-element.16), channel_id=1, source_target_pairs={{0,6},{1,7},{2,4},{3,5},{4,2},{5,3},{6,0},{7,1},{8,14},{9,15},{10,... | collective-permute-start | bytes 1966088 | tf_op jit(solution)/shard_map/ppermute | solution.py:244
Sparse Core Ops, SparseCore 0:
  10.8 104.3 reduce-scatter.1

commit v5 on v4

--- a/solution.py
+++ b/solution.py
@@ -9,7 +9,7 @@
 
 CAP = 5
 CHUNKS = 1
-STRIP = 256
+STRIP = 512
 VMEM_LIMIT = 48 * 1024 * 1024
 PRODUCT_VMEM_LIMIT = 32 * 1024 * 1024
 

time: 336 us -> 335 us (level)
  blocking collectives: 98.8 us -> 109 us
  Pallas kernels: 28.3 us -> 22.2 us
    all_to_all x2, blocking collectives: 98.8 us -> 109 us  [exchange(): lax.all_to_all(pieces, 'dp', split_axis=0, concat_axis=0, tiled=True)]
    pallas_call x1, Pallas kernels: 9.79 us -> 3.33 us  [collect(): pl.pallas_call(functools.partial(collect_kernel, len(sources), start), ou...]
where the time goes in v5:
time: 335 us; the launch traced here: 334 us
  waiting for transfers between devices  172 us (51%)
  blocking collectives  109 us (33%)
  Pallas kernels  22.2 us (7%)
  between operations  13.6 us (4%)
  starting transfers between devices  9.57 us (3%)
  local copies, waits for them, and re-layouts  4.27 us (1%)
    all_to_all x2, blocking collectives, exchange(): lax.all_to_all(pieces, 'dp', split_axis=0, concat_axis=0, tiled=True)  109 us
    reduce_scatter x1, waiting for transfers between devices, shards(): lax.psum_scatter(grad_partial, 'dp', scatter_dimension=2, tiled=True)[0]  107 us
    ppermute x11, waiting for transfers between devices, swap(): lax.ppermute(piece, 'group', [(g, g ^ distance) for g in range(groups)])  65 us
    pallas_call x1, Pallas kernels, precondition(): pl.pallas_call(precondition_kernel, out_shape=jax.ShapeDtypeStruct(pieces...  9.86 us
    ppermute x11, starting transfers between devices, swap(): lax.ppermute(piece, 'group', [(g, g ^ distance) for g in range(groups)])  9.57 us
  transfers between devices with their start and end apart: 12, of which 9 were waited for; matrix products, arithmetic and copies ran while one was open for 1% of the time, Pallas kernels for 0%

profile of v5, /device:TPU:0, one launch (start us, length us, event | category | flops | bytes accessed | tf_op | source)
XLA Modules:
  0.0 334.1 jit_solution(2643718790341329257)
XLA Ops:
  6.5 0.7 reduce-scatter.2.cloned.1.call-update
  7.4 0.2 convert_reduce_fusion
  7.8 0.4 select_reduce_fusion.1
  8.3 0.1 copy.14
  8.5 106.7 %reduce-scatter.2.cloned.1.call-done = bf16[1,7,64,1024]{3,2,1,0:T(8,128)(2,1)} async-done(((bf16[1,7,1024,1024]{3,2,1,0:T(8,128)(2,1)}), bf16[1,7,64,1024]{3,2,1,0:T(8,128)(2,1)}) %reduce-scatter.2.cloned.1.call-update) | async-done | bytes 917520 | tf_op jit(solution)/shard_map/reduce_scatter | solution.py:254
  115.2 1.2 copy-done
  116.3 2.7 spread.2
  119.0 1.9 collective-permute-start.1
  120.9 1.7 collective-permute-start.2
  122.6 1.2 collective-permute-start.3
  123.9 0.7 reshape.316
  124.9 12.0 %collective-permute-done.1.refs_2_ = bf16[5,64,1024]{2,1,0:T(8,128)(2,1)S(1)} collective-permute-done((bf16[5,64,1024]{2,1,0:T(8,128)(2,1)}, bf16[5,64,1024]{2,1,0:T(8,128)(2,1)S(1)}, u32[]{:S(2)}, u32[]{:S(2)}) %collective-permute-start.1) | collective-permute-done | bytes 655392 | tf_op jit(solution)/shard_map/ppermute | solution.py:244
  136.9 14.3 %collective-permute-done.2.refs_3_ = bf16[5,64,1024]{2,1,0:T(8,128)(2,1)S(1)} collective-permute-done((bf16[5,64,1024]{2,1,0:T(8,128)(2,1)}, bf16[5,64,1024]{2,1,0:T(8,128)(2,1)S(1)}, u32[]{:S(2)}, u32[]{:S(2)}) %collective-permute-start.2) | collective-permute-done | bytes 655392 | tf_op jit(solution)/shard_map/ppermute | solution.py:244
  151.2 2.4 collective-permute-done.3.refs_4_
  153.6 0.9 select_reduce_fusion.5
  154.5 0.7 pad_add_fusion.to_ref
  155.3 0.4 collective-permute-done.6.refs_7_
  155.7 1.2 copy-done.1
  156.9 3.3 collect.1
  160.2 55.8 %all_to_all.10 = bf16[16,128,1024]{2,1,0:T(8,128)(2,1)S(1)} all-to-all(bf16[16,128,1024]{2,1,0:T(8,128)(2,1)} %bitcast.10), channel_id=1, replica_groups=mesh['dp'=16,'group'=8] {'dp'}, dimensions={0} | all-to-all | bytes 8388608 | tf_op jit(solution)/shard_map/all_to_all | solution.py:238
  216.1 9.9 %precondition.1 = bf16[16,2,64,1024]{3,2,1,0:T(8,128)(2,1)S(1)} custom-call(bf16[2,1024,1024]{2,1,0:T(8,128)(2,1)S(1)} %copy-done.3, bf16[2,1024,1024]{2,1,0:T(8,128)(2,1)S(1)} %copy-done.4, bf16[16,2,64,1024]{3,2,1,0:T(8,128)(2,1)S(1)} %bitcast.5), custom_call_target="tpu_custom_call" | custom-call | flops 8589934592 | bytes 16777216 | tf_op jit(solution)/shard_map/precondition/pallas_call | solution.py:161
  225.9 53.6 %all_to_all.11 = bf16[16,128,1024]{2,1,0:T(8,128)(2,1)} all-to-all(bf16[16,128,1024]{2,1,0:T(8,128)(2,1)S(1)} %bitcast.6), channel_id=1, replica_groups=mesh['dp'=16,'group'=8] {'dp'}, dimensions={0} | all-to-all | bytes 8388608 | tf_op jit(solution)/shard_map/all_to_all | solution.py:238
  279.8 7.2 %collective-permute-done.7.refs_1_ = bf16[32,64,1024]{2,1,0:T(8,128)(2,1)} collective-permute-done((bf16[32,64,1024]{2,1,0:T(8,128)(2,1)}, bf16[32,64,1024]{2,1,0:T(8,128)(2,1)}, u32[]{:S(2)}, u32[]{:S(2)}) %collective-permute-start.7) | collective-permute-done | bytes 4194336 | tf_op jit(solution)/shard_map/ppermute | solution.py:244
  287.0 2.7 spread.3
  289.8 0.3 collective-permute-start.8
  290.1 1.4 collective-permute-start.9
  291.5 3.0 collective-permute-start.10
  294.7 0.1 slice_reduce_fusion.from_ref
  294.8 12.8 %collective-permute-done.8.refs_2_ = bf16[5,64,1024]{2,1,0:T(8,128)(2,1)S(1)} collective-permute-done((bf16[5,64,1024]{2,1,0:T(8,128)(2,1)}, bf16[5,64,1024]{2,1,0:T(8,128)(2,1)S(1)}, u32[]{:S(2)}, u32[]{:S(2)}) %collective-permute-start.8) | collective-permute-done | bytes 655392 | tf_op jit(solution)/shard_map/ppermute | solution.py:244
  307.6 13.2 %collective-permute-done.9.refs_3_ = bf16[5,64,1024]{2,1,0:T(8,128)(2,1)S(1)} collective-permute-done((bf16[5,64,1024]{2,1,0:T(8,128)(2,1)}, bf16[5,64,1024]{2,1,0:T(8,128)(2,1)S(1)}, u32[]{:S(2)}, u32[]{:S(2)}) %collective-permute-start.9) | collective-permute-done | bytes 655392 | tf_op jit(solution)/shard_map/ppermute | solution.py:244
  320.8 2.7 collective-permute-done.10.refs_4_
  323.5 3.7 %update.1 = f32[7,64,1024]{2,1,0:T(8,128)} custom-call(s32[5]{0:T(128)S(1)} %slice_reduce_fusion.from_ref, s32[20]{0:T(128)S(1)} %sub.68.to_ref, f32[7,64,1024]{2,1,0:T(8,128)S(1)} %copy-done.2, bf16[32,64,1024]{2,1,0:T(8,128)(2,1)} %bitcast.4.refs_0_, bf16[32,64,1024]{2,1,0:T(8,128)(2,1)} %collective-permute-done.7.refs_1_, ...), custom_call_target="tpu_custom_call" | custom-call | tf_op jit(solution)/shard_map/update/pallas_call | solution.py:215
  (52 shorter events, 1.3 us)
Async XLA Ops:
  6.5 0.8 copy-start.6
  6.5 108.6 %reduce-scatter.2.cloned.1.call-start = ((), (), s32[]{:S(2)}) async-start(), calls=%async_computation.3 | async-start | bytes 15597568 | tf_op jit(solution)/shard_map/reduce_scatter | solution.py:254
  7.4 0.8 copy-start.5
  7.6 0.6 copy-start.7
  115.2 1.2 copy-start
  119.0 17.9 %collective-permute-start.1 = (bf16[5,64,1024]{2,1,0:T(8,128)(2,1)}, bf16[5,64,1024]{2,1,0:T(8,128)(2,1)S(1)}, u32[]{:S(2)}, u32[]{:S(2)}) collective-permute-start(bf16[5,64,1024]{2,1,0:T(8,128)(2,1)} %get-tuple-element.11), channel_id=1, source_target_pairs={{0,2},{1,3},{2,0},{3,1},{4,6},{5,7},{6,4},{7,5},{8,10},{9,11},{10,... | collective-permute-start | bytes 1966088 | tf_op jit(solution)/shard_map/ppermute | solution.py:244
  120.9 30.3 %collective-permute-start.2 = (bf16[5,64,1024]{2,1,0:T(8,128)(2,1)}, bf16[5,64,1024]{2,1,0:T(8,128)(2,1)S(1)}, u32[]{:S(2)}, u32[]{:S(2)}) collective-permute-start(bf16[5,64,1024]{2,1,0:T(8,128)(2,1)} %get-tuple-element.12), channel_id=1, source_target_pairs={{0,4},{1,5},{2,6},{3,7},{4,0},{5,1},{6,2},{7,3},{8,12},{9,13},{10,... | collective-permute-start | bytes 1966088 | tf_op jit(solution)/shard_map/ppermute | solution.py:244
  122.6 31.0 %collective-permute-start.3 = (bf16[5,64,1024]{2,1,0:T(8,128)(2,1)S(1)}, bf16[5,64,1024]{2,1,0:T(8,128)(2,1)S(1)}, u32[]{:S(2)}, u32[]{:S(2)}) collective-permute-start(bf16[5,64,1024]{2,1,0:T(8,128)(2,1)S(1)} %get-tuple-element.13), channel_id=1, source_target_pairs={{0,6},{1,7},{2,4},{3,5},{4,2},{5,3},{6,0},{7,1},{8,14},{9,15},{10,... | collective-permute-start | bytes 1966088 | tf_op jit(solution)/shard_map/ppermute | solution.py:244
  124.6 30.6 %collective-permute-start = (bf16[7,64,1024]{2,1,0:T(8,128)(2,1)}, bf16[7,64,1024]{2,1,0:T(8,128)(2,1)S(1)}, u32[]{:S(2)}, u32[]{:S(2)}) collective-permute-start(bf16[7,64,1024]{2,1,0:T(8,128)(2,1)} %bitcast.7), channel_id=1, source_target_pairs={{0,1},{1,0},{2,3},{3,2},{4,5},{5,4},{6,7},{7,6},{8,9},{9,8},{10,11... | collective-permute-start | bytes 2752520 | tf_op jit(solution)/shard_map/ppermute | solution.py:244
  136.9 18.3 %collective-permute-start.4 = (bf16[5,64,1024]{2,1,0:T(8,128)(2,1)S(1)}, bf16[5,64,1024]{2,1,0:T(8,128)(2,1)S(1)}, u32[]{:S(2)}, u32[]{:S(2)}) collective-permute-start(bf16[5,64,1024]{2,1,0:T(8,128)(2,1)S(1)} %collective-permute-done.1.refs_2_), channel_id=1, source_target_pairs={{0,1},{1,0},{2,3},{3,2},{4,5},{5,4},{6,7},{7,6},{8,9},{9,8},{10,11... | collective-permute-start | bytes 1966088 | tf_op jit(solution)/shard_map/ppermute | solution.py:244
  151.2 4.0 %collective-permute-start.5 = (bf16[5,64,1024]{2,1,0:T(8,128)(2,1)S(1)}, bf16[5,64,1024]{2,1,0:T(8,128)(2,1)S(1)}, u32[]{:S(2)}, u32[]{:S(2)}) collective-permute-start(bf16[5,64,1024]{2,1,0:T(8,128)(2,1)S(1)} %collective-permute-done.2.refs_3_), channel_id=1, source_target_pairs={{0,1},{1,0},{2,3},{3,2},{4,5},{5,4},{6,7},{7,6},{8,9},{9,8},{10,11... | collective-permute-start | bytes 1966088 | tf_op jit(solution)/shard_map/ppermute | solution.py:244
  153.6 2.1 collective-permute-start.6
  155.7 1.2 copy-start.1
  160.2 55.9 %copy-start.3 = (bf16[2,1024,1024]{2,1,0:T(8,128)(2,1)S(1)}, bf16[2,1024,1024]{2,1,0:T(8,128)(2,1)}, u32[]{:S(2)}) copy-start(bf16[2,1024,1024]{2,1,0:T(8,128)(2,1)} %left_ref.1) | copy-start | bytes 12582916
  160.2 55.9 %copy-start.4 = (bf16[2,1024,1024]{2,1,0:T(8,128)(2,1)S(1)}, bf16[2,1024,1024]{2,1,0:T(8,128)(2,1)}, u32[]{:S(2)}) copy-start(bf16[2,1024,1024]{2,1,0:T(8,128)(2,1)} %right_ref.1) | copy-start | bytes 12582916
  279.5 7.5 %collective-permute-start.7 = (bf16[32,64,1024]{2,1,0:T(8,128)(2,1)}, bf16[32,64,1024]{2,1,0:T(8,128)(2,1)}, u32[]{:S(2)}, u32[]{:S(2)}) collective-permute-start(bf16[32,64,1024]{2,1,0:T(8,128)(2,1)} %bitcast.4.refs_0_), channel_id=1, source_target_pairs={{0,1},{1,0},{2,3},{3,2},{4,5},{5,4},{6,7},{7,6},{8,9},{9,8},{10,11... | collective-permute-start | bytes 12582920 | tf_op jit(solution)/shard_map/ppermute | solution.py:244
  279.8 43.7 %copy-start.2 = (f32[7,64,1024]{2,1,0:T(8,128)S(1)}, f32[7,64,1024]{2,1,0:T(8,128)}, u32[]{:S(2)}) copy-start(f32[7,64,1024]{2,1,0:T(8,128)} %momentum_ref.1) | copy-start | bytes 5505028
  289.8 17.9 %collective-permute-start.8 = (bf16[5,64,1024]{2,1,0:T(8,128)(2,1)}, bf16[5,64,1024]{2,1,0:T(8,128)(2,1)S(1)}, u32[]{:S(2)}, u32[]{:S(2)}) collective-permute-start(bf16[5,64,1024]{2,1,0:T(8,128)(2,1)} %get-tuple-element.14), channel_id=1, source_target_pairs={{0,2},{1,3},{2,0},{3,1},{4,6},{5,7},{6,4},{7,5},{8,10},{9,11},{10,... | collective-permute-start | bytes 1966088 | tf_op jit(solution)/shard_map/ppermute | solution.py:244
  290.1 30.8 %collective-permute-start.9 = (bf16[5,64,1024]{2,1,0:T(8,128)(2,1)}, bf16[5,64,1024]{2,1,0:T(8,128)(2,1)S(1)}, u32[]{:S(2)}, u32[]{:S(2)}) collective-permute-start(bf16[5,64,1024]{2,1,0:T(8,128)(2,1)} %get-tuple-element.15), channel_id=1, source_target_pairs={{0,4},{1,5},{2,6},{3,7},{4,0},{5,1},{6,2},{7,3},{8,12},{9,13},{10,... | collective-permute-start | bytes 1966088 | tf_op jit(solution)/shard_map/ppermute | solution.py:244
  291.5 32.0 %collective-permute-start.10 = (bf16[5,64,1024]{2,1,0:T(8,128)(2,1)}, bf16[5,64,1024]{2,1,0:T(8,128)(2,1)}, u32[]{:S(2)}, u32[]{:S(2)}) collective-permute-start(bf16[5,64,1024]{2,1,0:T(8,128)(2,1)} %get-tuple-element.16), channel_id=1, source_target_pairs={{0,6},{1,7},{2,4},{3,5},{4,2},{5,3},{6,0},{7,1},{8,14},{9,15},{10,... | collective-permute-start | bytes 1966088 | tf_op jit(solution)/shard_map/ppermute | solution.py:244
Sparse Core Ops, SparseCore 0:
  10.8 104.3 reduce-scatter.1
